TPU v7x, 128 devices: a whole 4x4x4 slice. The times are simulated.
128 devices in a mesh: rows: 32 (over x, z, core), cols: 4 (over y).
Axes of the slice: x: 4, y: 4, z: 4, core: 2. Of those that a mesh axis runs over, the one named last changes fastest.
Arguments:
- momentum: bfloat16 [12288, 26624], P('rows', 'cols'), may hold values from -30 to 30
- gradient: bfloat16 [12288, 26624], P('rows', 'cols'), may hold values from -3 to 3
- basis: bfloat16 [512, 26624], P('rows', 'cols')
Outputs:
- momentum_new: bfloat16 [12288, 26624], P('rows', 'cols')
- basis_new: bfloat16 [512, 26624], P('rows', 'cols')
- update: bfloat16 [12288, 26624], P('rows', 'cols')
All inputs are finite; a program needn't handle non-finite values.
Results may differ from a plain program's by a relative error of at most 0.027.
Values may be sent and summed in bfloat16 or wider, within the bound.
A program may use at most 128 MiB of HBM per device.

v0:
```python
import math

import jax
import jax.numpy as jnp
from jax import lax
from jax.sharding import PartitionSpec as P

ROWS = 12288
WIDTH = 26624
RANK = 512


def local(momentum, gradient, basis):
    buffer = (momentum.astype(jnp.float32) + gradient.astype(jnp.float32)).astype(jnp.bfloat16)
    partial_left = lax.dot_general(
        buffer,
        lax.all_gather(basis, "rows", axis=0, tiled=True),
        (((1,), (1,)), ((), ())),
        preferred_element_type=jnp.float32,
    )
    left = lax.psum(partial_left.astype(jnp.bfloat16), "cols").astype(jnp.float32)
    gram_local = lax.dot_general(
        left, left, (((0,), (0,)), ((), ())), precision=lax.Precision.HIGHEST
    )
    gram = lax.psum(gram_local.astype(jnp.bfloat16), "rows").astype(jnp.float32)
    lower = jnp.linalg.cholesky(gram)
    ortho = jax.scipy.linalg.solve_triangular(lower, left.T, lower=True).T.astype(jnp.bfloat16)
    share = basis.shape[0]
    local_right = lax.dot_general(
        ortho, buffer, (((0,), (0,)), ((), ())), preferred_element_type=jnp.float32
    )
    right = lax.psum(local_right.astype(jnp.bfloat16), "rows")
    right_wide = right.astype(jnp.float32)
    squares = lax.psum(jnp.sum(right_wide * right_wide, axis=1), "cols")
    norms = jnp.sqrt(squares + 1e-06)
    basis_full = (right_wide / norms[:, None]).astype(jnp.bfloat16)
    basis_new = lax.dynamic_slice_in_dim(basis_full, lax.axis_index("rows") * share, share, 0)
    feedback = jnp.dot(ortho, right, preferred_element_type=jnp.float32)
    momentum_new = (buffer.astype(jnp.float32) - 0.2 * feedback).astype(jnp.bfloat16)
    factor = math.sqrt(ROWS * WIDTH / RANK)
    update = (factor * jnp.dot(ortho, basis_full, preferred_element_type=jnp.float32)).astype(
        jnp.bfloat16
    )
    return (momentum_new, basis_new, update)


def solution(mesh):
    return jax.shard_map(
        local,
        mesh=mesh,
        in_specs=(P("rows", "cols"), P("rows", "cols"), P("rows", "cols")),
        out_specs=(P("rows", "cols"), P("rows", "cols"), P("rows", "cols")),
        check_vma=False,
    )
```

profile of v0, /device:TPU:1, one launch (start us, length us, event | category | flops | bytes accessed | tf_op | source)
XLA Modules:
  0.0 526.8 jit_solution(7393689816988952809)
XLA Ops:
  7.2 0.0 all-gather.2.cloned.1.call-start
  7.2 0.7 all-gather.2.cloned.1.call-update
  7.9 0.0 all-reduce.5.cloned.1.call-start
  7.9 56.1 %all-gather.2.cloned.1.call-done = bf16[512,6656]{1,0:T(8,128)(2,1)} async-done(((bf16[16,6656]{1,0:T(8,128)(2,1)}), bf16[512,6656]{1,0:T(8,128)(2,1)}) %all-gather.2.cloned.1.call-update) | async-done | bytes 6815760 | tf_op jit(solution)/shard_map/all_gather | solution.py:17
  64.0 9.5 %convolution_convert_fusion.2 = bf16[384,512]{1,0:T(8,128)(2,1)} fusion(bf16[512,6656]{1,0:T(8,128)(2,1)} %all-gather.2.cloned.1.call-done, bf16[384,6656]{1,0:T(8,128)(2,1)} %param.4, bf16[384,6656]{1,0:T(8,128)(2,1)} %param.3), kind=kOutput, calls=%fused_computation.13 | convolution fusion | flops 2627665920 | bytes 17432576 | tf_op jit(solution)/shard_map/dot_general | solution.py:15
  73.6 0.0 all-reduce.5.cloned.1.call-update
  73.6 0.0 all-reduce.7.cloned.1.call-start
  73.6 38.6 %all-reduce.5.cloned.1.call-done = bf16[384,512]{1,0:T(8,128)(2,1)} async-done(((bf16[384,512]{1,0:T(8,128)(2,1)}), bf16[384,512]{1,0:T(8,128)(2,1)}) %all-reduce.5.cloned.1.call-update) | async-done | bytes 393232 | tf_op jit(solution)/shard_map/psum | solution.py:21
  112.2 2.4 convolution_convert_fusion.1
  114.6 0.0 all-reduce.7.cloned.1.call-update
  114.6 0.6 all-reduce.9.cloned.1.call-start
  115.2 1.1 bitcast_convert_fusion
  116.3 106.4 %all-reduce.7.cloned.1.call-done = bf16[512,512]{0,1:T(8,128)(2,1)} async-done(((bf16[512,512]{0,1:T(8,128)(2,1)}), bf16[512,512]{0,1:T(8,128)(2,1)}) %all-reduce.7.cloned.1.call-update) | async-done | bytes 524304 | tf_op jit(solution)/shard_map/psum | solution.py:25
  222.7 1.3 copy.7
  224.0 1.2 fusion.3
  225.2 11.7 %cholesky.104 = f32[128,128]{1,0:T(8,128)S(1)} custom-call(f32[128,128]{1,0:T(8,128)S(1)} %cholesky.266), custom_call_target="Cholesky" | custom-call | tf_op jit(solution)/shard_map/jit(cholesky)/cholesky | solution.py:26
  236.9 0.1 cholesky.224
  237.1 9.8 %custom-call.31 = f32[1,128,128]{1,2,0:T(8,128)S(1)} custom-call(f32[1,128,128]{2,1,0:T(8,128)S(1)} %get-tuple-element.30), custom_call_target="InvertDiagBlocksLowerTriangular" | custom-call | tf_op jit(solution)/shard_map/jit(cholesky)/cholesky | solution.py:26
  246.9 0.3 constant_dynamic-update-slice_fusion.3
  247.2 0.3 convolution_subtract_fusion.3
  247.6 11.7 %cholesky.217 = f32[128,128]{1,0:T(8,128)S(1)} custom-call(f32[128,128]{1,0:T(8,128)S(1)} %cholesky.270), custom_call_target="Cholesky" | custom-call | tf_op jit(solution)/shard_map/jit(cholesky)/cholesky | solution.py:26
  259.3 10.0 %custom-call.32 = f32[1,128,128]{1,2,0:T(8,128)S(1)} custom-call(f32[1,128,128]{2,1,0:T(8,128)S(1)} %get-tuple-element.27), custom_call_target="InvertDiagBlocksLowerTriangular" | custom-call | tf_op jit(solution)/shard_map/jit(cholesky)/cholesky | solution.py:26
  269.3 0.3 convolution_dynamic-update-slice_fusion
  269.5 0.4 convolution_subtract_fusion.4
  269.9 11.7 %cholesky.238 = f32[128,128]{1,0:T(8,128)S(1)} custom-call(f32[128,128]{1,0:T(8,128)S(1)} %cholesky.275), custom_call_target="Cholesky" | custom-call | tf_op jit(solution)/shard_map/jit(cholesky)/cholesky | solution.py:26
  281.7 9.8 %custom-call.33 = f32[1,128,128]{1,2,0:T(8,128)S(1)} custom-call(f32[1,128,128]{2,1,0:T(8,128)S(1)} %get-tuple-element.24), custom_call_target="InvertDiagBlocksLowerTriangular" | custom-call | tf_op jit(solution)/shard_map/jit(cholesky)/cholesky | solution.py:26
  291.5 0.2 convolution_dynamic-update-slice_fusion.1
  291.7 0.4 convolution_subtract_fusion.5
  292.1 11.7 %cholesky.255 = f32[128,128]{1,0:T(8,128)S(1)} custom-call(f32[128,128]{1,0:T(8,128)S(1)} %convolution_subtract_fusion.5), custom_call_target="Cholesky" | custom-call | tf_op jit(solution)/shard_map/jit(cholesky)/cholesky | solution.py:26
  303.9 0.7 compare_reduce_fusion.1
  304.6 0.6 compare_reduce_fusion
  305.2 0.6 compare_reduce_fusion.2
  308.4 0.1 select_select_fusion
  308.5 8.2 %while.1 = (s32[]{:T(128)}, f32[512,512]{1,0:T(8,128)S(1)}, s32[4,2]{0,1:T(2,128)S(1)}, f32[4,128,128]{2,1,0:T(8,128)S(1)}, s32[]{:T(128)}) while((s32[]{:T(128)}, f32[512,512]{1,0:T(8,128)S(1)}, s32[4,2]{0,1:T(2,128)S(1)}, f32[4,128,128]{2,1,0:T(8,128)S(1)}, s32[]{:T(128)}) %tuple.34), condition=%wide.while_cond, body=%wide.while_body.sunk | while | flops 2 | bytes 131189 | solution.py:27
  308.8 0.1 constant_dynamic-slice_fusion.3
  308.8 0.5 fusion.47
  309.4 1.4 bitcast_dynamic-update-slice_fusion.2
  310.8 0.1 constant_dynamic-slice_fusion.3
  310.8 0.5 fusion.47
  311.4 1.4 bitcast_dynamic-update-slice_fusion.2
  312.8 0.1 constant_dynamic-slice_fusion.3
  312.8 0.5 fusion.47
  313.4 1.4 bitcast_dynamic-update-slice_fusion.2
  314.8 0.1 constant_dynamic-slice_fusion.3
  314.8 0.5 fusion.47
  315.4 1.4 bitcast_dynamic-update-slice_fusion.2
  316.8 39.3 %custom-call.34 = f32[4,128,128]{1,2,0:T(8,128)S(1)} custom-call(f32[4,128,128]{2,1,0:T(8,128)S(1)} %get-tuple-element.10), custom_call_target="InvertDiagBlocksLowerTriangular" | custom-call | tf_op jit(solution)/shard_map/jit(_solve_triangular)/triangular_solve | solution.py:27
  356.1 1.2 fusion.35
  357.3 0.5 convolution_subtract_fusion.2
  357.8 0.4 fusion.34
  358.2 0.8 convolution_subtract_fusion.1
  359.0 0.4 fusion.33
  359.4 1.1 convolution_subtract_fusion
  360.6 0.4 convolution_convert_fusion.3
  361.0 10.5 %convolution_convert_fusion = bf16[512,6656]{1,0:T(8,128)(2,1)} fusion(bf16[128,384]{1,0:T(8,128)(2,1)S(1)} %convolution_convert_fusion.3, bf16[128,384]{1,0:T(8,128)(2,1)S(1)} %get-tuple-element.33, bf16[128,384]{1,0:T(8,128)(2,1)S(1)} %get-tuple-element.35, bf16[128,384]{1,0:T(8,128)(2,1)S(1)} %get-tuple-element.37, bf16[384,6656]{1,0:T(8,128)(2,1)} %param.4, ...), kind=kOutput, calls=%fused_computation.8 | convolution fusion | flops 2632450048 | bytes 17432576 | tf_op jit(solution)/shard_map/dot_general | solution.py:29
  371.5 0.0 all-reduce.9.cloned.1.call-update
  371.5 116.9 %all-reduce.9.cloned.1.call-done = bf16[512,6656]{1,0:T(8,128)(2,1)} async-done(((bf16[512,6656]{1,0:T(8,128)(2,1)}), bf16[512,6656]{1,0:T(8,128)(2,1)}) %all-reduce.9.cloned.1.call-update) | async-done | bytes 6815760 | tf_op jit(solution)/shard_map/psum | solution.py:32
  488.4 4.5 fusion
  492.9 8.7 %psum.31 = f32[512]{0:T(512)S(1)} all-reduce(f32[512]{0:T(512)S(1)} %fusion), channel_id=1, replica_groups=mesh['rows'=32,'cols'=4] {'cols'}, use_global_device_ids=true, to_apply=%region_12.13 | all-reduce | flops 512 | bytes 4096 | tf_op jit(solution)/shard_map/psum | solution.py:34
  501.6 5.3 %fusion.1 = bf16[512,6656]{1,0:T(8,128)(2,1)S(1)} fusion(bf16[512,6656]{1,0:T(8,128)(2,1)} %all-reduce.9.cloned.1.call-done, f32[512]{0:T(512)S(1)} %add_sqrt_fusion), kind=kLoop, calls=%fused_computation.5 | loop fusion | flops 10223616 | bytes 13633536 | tf_op jit(solution)/shard_map/convert_element_type | solution.py:36
  506.9 4.6 fusion.2
  511.4 0.7 constant_dynamic-slice_fusion.1
  512.1 0.0 slice-done
  512.2 7.9 %subtract_convert_fusion = bf16[384,6656]{1,0:T(8,128)(2,1)} fusion(bf16[512,6656]{1,0:T(8,128)(2,1)S(1)} %bitcast.62, bf16[128,384]{1,0:T(8,128)(2,1)S(1)} %convolution_convert_fusion.3, bf16[128,384]{1,0:T(8,128)(2,1)S(1)} %get-tuple-element.33, bf16[128,384]{1,0:T(8,128)(2,1)S(1)} %get-tuple-element.35, bf16[128,384]{1,0:T(8,128)(2,1)S(1)} %get-tuple-element.37, ...), kind=kOutput, calls=%fused_computation.9 | convolution fusion | flops 2639265792 | bytes 22544384 | tf_op jit(solution)/shard_map/dot_general | solution.py:38
  (15 shorter events, 0.2 us)
Async XLA Ops:
  7.2 56.9 %all-gather.2.cloned.1.call-start = ((), (), s32[]{:S(2)}) async-start(), calls=%async_computation | async-start | bytes 7028736 | tf_op jit(solution)/shard_map/all_gather | solution.py:17
  7.9 104.3 %all-reduce.5.cloned.1.call-start = ((), (), s32[]{:S(2)}) async-start(), calls=%async_computation.1 | async-start | bytes 786432 | tf_op jit(solution)/shard_map/psum | solution.py:21
  73.6 149.1 %all-reduce.7.cloned.1.call-start = ((), (), s32[]{:S(2)}) async-start(), calls=%async_computation.2 | async-start | bytes 1048576 | tf_op jit(solution)/shard_map/psum | solution.py:25
  114.6 373.7 %all-reduce.9.cloned.1.call-start = ((), (), s32[]{:S(2)}) async-start(), calls=%async_computation.3 | async-start | bytes 13631488 | tf_op jit(solution)/shard_map/psum | solution.py:32
  488.4 23.8 %slice-start = ((s8[6815744]{0:T(1024)(128)(4,1)}), s8[2621440]{0:T(1024)(128)(4,1)S(1)}, s32[]{:S(2)}) async-start(s8[6815744]{0:T(1024)(128)(4,1)} %bitcast.61), calls=%async_computation.4 | async-start | bytes 5242880
  501.6 10.6 %slice-start.1 = ((s8[6815744]{0:T(1024)(128)(4,1)}), s8[4194304]{0:T(1024)(128)(4,1)S(1)}, s32[]{:S(2)}) async-start(s8[6815744]{0:T(1024)(128)(4,1)} %bitcast.61), calls=%async_computation.5 | async-start | bytes 8388608
Sparse Core Ops, SparseCore 0:
  10.3 53.7 all-gather.1
  73.7 38.4 all-reduce.4
  116.3 106.3 all-reduce.6
  371.6 116.7 all-reduce.8
where the time goes:
time: 532 us; the launch traced here: 527 us
  waiting for transfers between devices  319 us (60%)
  other arithmetic  130 us (24%)
  matrix products  41.5 us (8%)
  between operations  16.8 us (3%)
  local copies, waits for them, and re-layouts  10 us (2%)
  blocking collectives  8.69 us (2%)
    psum x1, waiting for transfers between devices, local(): right = lax.psum(local_right.astype(jnp.bfloat16), 'rows')  117 us
    psum x1, waiting for transfers between devices, local(): gram = lax.psum(gram_local.astype(jnp.bfloat16), 'rows').astype(jnp.float32)  106 us
    another operation x14, other arithmetic, local(): lower = jnp.linalg.cholesky(gram)  78.5 us
    all_gather x1, waiting for transfers between devices, local(): lax.all_gather(basis, 'rows', axis=0, tiled=True)  56.1 us
    another operation x3, other arithmetic, local(): jax.scipy.linalg.solve_triangular(lower, left.T, lower=True)  39.4 us
    psum x1, waiting for transfers between devices, local(): lax.psum(partial_left.astype(jnp.bfloat16), 'cols').astype(jnp.float32)  38.6 us
  transfers between devices with their start and end apart: 4, of which 4 were waited for; matrix products, arithmetic and copies ran while one was open for 0% of the time, Pallas kernels for 0%

commit v1 on v0

v1 whole, which is shorter than its diff:
```python
import functools
import math

import jax
import jax.numpy as jnp
from jax import lax
from jax.experimental import pallas as pl
from jax.experimental.pallas import tpu as pltpu
from jax.sharding import PartitionSpec as P

ROWS = 12288
WIDTH = 26624
RANK = 512
MESH = pl.DeviceIdType.MESH
BF = jnp.bfloat16
F32 = jnp.float32

LOCAL = 384
COLS = 6656
HALF = 3328
PART = 1664
SEG = 832
SUB = 208
B = 128
N_SEMS = 192


def mod4(v):
    return lax.rem(v + 4, 4)


def rows_at(start, size, unit=16):
    return pl.ds(pl.multiple_of(start, unit), size)


def dotp(a, b, dims):
    return lax.dot_general(
        a, b, (dims, ((), ())), precision=lax.Precision.HIGHEST, preferred_element_type=F32
    )


def dotb(a, b, dims):
    return lax.dot_general(a, b, (dims, ((), ())), preferred_element_type=F32)


def split(a):
    hi = a.astype(BF)
    return hi, (a - hi.astype(F32)).astype(BF)


def sweep(w_ref, t, hook):
    sub = lax.broadcasted_iota(jnp.int32, (8, B), 0)
    lane = lax.broadcasted_iota(jnp.int32, (8, B), 1)
    panels = B // 8
    for p in range(panels):
        top = t[:8]
        cols = jnp.stack(
            [jnp.broadcast_to(top[:, 8 * p + j : 8 * p + j + 1], (8, B)) for j in range(8)]
        )
        for j in range(8):
            inv = lax.rsqrt(jnp.broadcast_to(cols[j, j : j + 1, :], (8, B)))
            below = jnp.where(sub > j, cols[j] * inv, 0.0)
            own = jnp.where(sub > j, 0.0, jnp.where(sub == j, 1.0, cols[j]))
            parts = [cols[:j]] if j else []
            parts.append(own[None])
            if j < 7:
                parts.append(cols[j + 1 :])
            cols = jnp.concatenate(parts, axis=0)
            row = cols[:, j : j + 1, :] * inv[None]
            cols = jnp.where((sub == j)[None], row, cols - below[None] * row)
        tri = [jnp.where(sub >= k, cols[k], 0.0) for k in range(8)]
        inside = (lane >= 8 * p) & (lane < 8 * p + 8)
        eye = jnp.where(inside, jnp.where(lane - 8 * p == sub, 1.0, 0.0), top)
        new = tri[0] * eye[0:1]
        for k in range(1, 8):
            new = new + tri[k] * eye[k : k + 1]
        w_ref[8 * p : 8 * p + 8, :] = jnp.where(lane <= sub + 8 * p, new, 0.0)
        if p < panels - 1:
            rest = t[8:]
            lanes = lax.broadcasted_iota(jnp.int32, rest.shape, 1)
            t = jnp.where((lanes >= 8 * p) & (lanes < 8 * p + 8), 0.0, rest)
            for k in range(8):
                y = jnp.sum(tri[k] * new, axis=0, keepdims=True)
                t = t - rest[:, 8 * p + k : 8 * p + k + 1] * y
        if p % 4 == 3:
            hook(p // 4)


def chol_inv(t_ref, w_ref, hook):
    lanes = lax.broadcasted_iota(jnp.int32, (B, RANK), 1)
    subs = lax.broadcasted_iota(jnp.int32, (B, RANK), 0)

    def block(k, carry):
        base = pl.multiple_of(k * B, B)
        rows = pl.ds(base, B)
        sweep(w_ref, t_ref[rows, rows], functools.partial(hook, k))
        own = (lanes >= base) & (lanes < base + B)
        mine = jnp.where(own, jnp.where(lanes - base == subs, 1.0, 0.0), t_ref[rows, :])
        new = dotp(w_ref[...], mine, ((1,), (0,)))
        t_ref[rows, :] = new

        def below(i, c):
            at = pl.ds(pl.multiple_of(i * B, B), B)
            t_ref[at, :] = jnp.where(own, 0.0, t_ref[at, :]) - dotp(
                t_ref[rows, at], new, ((0,), (0,))
            )
            return c

        lax.fori_loop(k + 1, RANK // B, below, 0)
        return carry

    lax.fori_loop(0, RANK // B, block, 0)


def gather_kernel(
    m_hbm, g_hbm, basis_hbm, zt_hbm, lhs_ref,
    mbuf, gbuf, sbuf, buf2, buf2t, bas, pleft, psend, precv, cp, yrh, yrf, left2,
    gs, gr, gram, tmat, wmat, zp, zown, zrh, zrf, zr2, zfull, nr1, nr2,
    load_sem, send_sem, recv_sem,
):
    r = lax.axis_index("rows")
    y = lax.axis_index("cols")
    c = lax.rem(r, 2)
    z = lax.rem(lax.div(r, 2), 4)
    x = lax.div(r, 8)
    p1 = x * (1 - c) + z * c
    p2 = z * (1 - c) + x * c

    def chip(a, b):
        return a * (4 - 3 * c) + b * (1 + 3 * c)

    def device(a, b):
        return 2 * chip(a, b) + c

    sib = (r + 1 - 2 * c, y)
    a1p = (device(mod4(p1 + 1), p2), y)
    a1m = (device(mod4(p1 - 1), p2), y)
    a2p = (device(p1, mod4(p2 + 1)), y)
    a2m = (device(p1, mod4(p2 - 1)), y)
    yp = (r, mod4(y + 1))
    ym = (r, mod4(y - 1))
    plane = [(dx, dz) for dx in range(4) for dz in range(4) if dx or dz]

    def peer(dx, dz):
        return (mod4(x + dx) * 8 + mod4(z + dz) * 2 + c, y)

    def source_chip(dx, dz):
        return mod4(x - dx) * 4 + mod4(z - dz)

    group = [(dy, dc) for dy in range(4) for dc in range(2) if dy or dc]

    def member(dy, dc):
        return (r + dc * (1 - 2 * c), mod4(y + dy))

    count = [0]
    sent = []

    def plan(src, dst, to, landing):
        i = count[0]
        count[0] += 1

        def copy(s, d):
            return pltpu.make_async_remote_copy(
                s, d, send_sem.at[i], recv_sem.at[i], device_id=to, device_id_type=MESH
            )

        sent.append(lambda: copy(src, dst).wait_send())
        return (lambda: copy(src, dst).start()), (lambda: copy(landing, landing).wait_recv())

    def send(src, dst, to, landing):
        start, wait = plan(src, dst, to, landing)
        start()
        return wait

    def columns(core, part):
        return pl.ds(pl.multiple_of(core * HALF + part * PART, 128), PART)

    order = [(1 - c, 0), (1 - c, 1), (c, 0), (c, 1)]

    def load(n):
        at = columns(*order[n])
        return [
            pltpu.make_async_copy(m_hbm.at[:, at], mbuf.at[n % 2], load_sem.at[2 * n]),
            pltpu.make_async_copy(g_hbm.at[:, at], gbuf.at[n % 2], load_sem.at[2 * n + 1]),
        ]

    loads = [load(n) for n in range(4)]
    for n in range(2):
        for copy in loads[n]:
            copy.start()
    own_rows = rows_at(r * 16, 16)
    parts = [pl.ds(0, PART), pl.ds(PART, PART)]
    own_basis = [
        pltpu.make_async_copy(
            basis_hbm.at[:, columns(c, n)], bas.at[own_rows, parts[n]], load_sem.at[8 + n]
        )
        for n in range(2)
    ]
    for copy in own_basis:
        copy.start()

    barrier = pltpu.get_barrier_semaphore()
    others = [peer(*d) for d in plane] + [member(*d) for d in group]
    for to in others:
        pl.semaphore_signal(barrier, inc=1, device_id=to, device_id_type=MESH)
    pl.semaphore_wait(barrier, len(others))

    sib_rows = rows_at((r + 1 - 2 * c) * 16, 16)
    got = [
        send(
            basis_hbm.at[:, columns(1 - c, n)],
            bas.at[own_rows, parts[n]],
            sib,
            bas.at[sib_rows, parts[n]],
        )
        for n in range(2)
    ]

    def piece(a, b, n):
        return bas.at[rows_at(chip(a, b) * 32, 32), parts[n]]

    def half_piece(a, b, n, h):
        return bas.at[rows_at(chip(a, b) * 32 + 16 * h, 16), parts[n]]

    def at1(d):
        return mod4(p1 + d)

    def at2(d):
        return mod4(p2 + d)

    first = []
    for n in range(2):
        own_basis[n].wait()
        got[n]()
        mine = piece(p1, p2, n)
        first.append(
            (
                send(mine, mine, a1p, piece(at1(-1), p2, n)),
                send(mine, mine, a1m, piece(at1(1), p2, n)),
            )
        )

    def both2(a, n):
        ref = piece(a, p2, n)
        return (
            send(ref, ref, a2p, piece(a, at2(-1), n)),
            send(ref, ref, a2m, piece(a, at2(1), n)),
        )

    def add_loaded(n, dst, row0, col0):
        for copy in loads[n]:
            copy.wait()

        def step(i, carry):
            at = rows_at(i * 16, 16)
            total = mbuf[n % 2, at, :].astype(F32) + gbuf[n % 2, at, :].astype(F32)
            dst[rows_at(row0 + i * 16, 16), pl.ds(col0, PART)] = total.astype(BF)
            return carry

        lax.fori_loop(0, LOCAL // 16, step, 0)
        if n < 2:
            for copy in loads[n + 2]:
                copy.start()

    my_rows = rows_at(c * LOCAL, LOCAL, 128)
    sib_side = rows_at((1 - c) * LOCAL, LOCAL, 128)

    def send_buffer(n):
        return send(
            sbuf.at[:, parts[n]], buf2.at[my_rows, parts[n]], sib, buf2.at[sib_side, parts[n]]
        )

    def turn(n, core):
        side = rows_at(core * LOCAL, LOCAL, 128)

        def step(i, carry):
            at = rows_at(n * PART + i * 128, 128, 128)
            buf2t[at, side] = buf2[side, at].T
            return carry

        lax.fori_loop(0, PART // 128, step, 0)

    add_loaded(0, sbuf, 0, 0)
    swapped = [send_buffer(0)]
    second = [[], []]
    opposite1 = []
    for n in range(2):
        from_m, from_p = first[n]
        second[n].append(both2(p1, n))
        from_m()
        ref = half_piece(at1(-1), p2, n, 0)
        opp0 = send(ref, ref, a1p, half_piece(at1(2), p2, n, 0))
        second[n].append(both2(at1(-1), n))
        from_p()
        ref = half_piece(at1(1), p2, n, 1)
        opp1 = send(ref, ref, a1m, half_piece(at1(2), p2, n, 1))
        second[n].append(both2(at1(1), n))
        opposite1.append((opp0, opp1))
    add_loaded(1, sbuf, 0, PART)
    swapped.append(send_buffer(1))
    for n in range(2):
        for wait in opposite1[n]:
            wait()
        second[n].append(both2(at1(2), n))
    add_loaded(2, buf2, c * LOCAL, 0)
    last = [[], []]
    offsets = (0, -1, 1, 2)

    def forward2(n, q):
        a = at1(offsets[q])
        from_m, from_p = second[n][q]
        from_m()
        ref = half_piece(a, at2(-1), n, 0)
        last[n].append(send(ref, ref, a2p, half_piece(a, at2(2), n, 0)))
        from_p()
        ref = half_piece(a, at2(1), n, 1)
        last[n].append(send(ref, ref, a2m, half_piece(a, at2(2), n, 1)))

    forward2(0, 0)
    forward2(0, 1)
    add_loaded(3, buf2, c * LOCAL, PART)
    forward2(0, 2)
    forward2(0, 3)
    forward2(1, 0)
    turn(0, c)
    forward2(1, 1)
    turn(1, c)
    swapped[0]()
    turn(0, 1 - c)
    forward2(1, 2)
    swapped[1]()
    turn(1, 1 - c)
    forward2(1, 3)

    for wait in last[0]:
        wait()
    pleft[sib_side, :] = dotb(buf2[sib_side, parts[0]], bas[:, parts[0]], ((1,), (1,)))
    pleft[my_rows, :] = dotb(buf2[my_rows, parts[0]], bas[:, parts[0]], ((1,), (1,)))
    for wait in last[1]:
        wait()
    psend[...] = (
        pleft[sib_side, :] + dotb(buf2[sib_side, parts[1]], bas[:, parts[1]], ((1,), (1,)))
    ).astype(BF)
    paired = send(psend, precv, sib, precv)
    pleft[my_rows, :] += dotb(buf2[my_rows, parts[1]], bas[:, parts[1]], ((1,), (1,)))
    paired()

    def ring_sum(plus, minus, size, value, out, half_in, full_in, between):
        half = size // 2

        def put(d, h, extra):
            v = value(d, h)
            if extra is not None:
                v = v + extra[...].astype(F32)
            slot = out.at[d % 4, h]
            slot[...] = v.astype(BF)
            return slot

        h0 = send(put(2, 0, None), half_in.at[0], plus, half_in.at[0])
        h1 = send(put(2, 1, None), half_in.at[1], minus, half_in.at[1])
        waits = [
            send(put(1, 1, None), full_in.at[0, 1], plus, full_in.at[0, 1]),
            send(put(-1, 0, None), full_in.at[1, 0], minus, full_in.at[1, 0]),
        ]
        between()
        h0()
        waits.append(send(put(1, 0, half_in.at[0]), full_in.at[0, 0], plus, full_in.at[0, 0]))
        h1()
        waits.append(send(put(-1, 1, half_in.at[1]), full_in.at[1, 1], minus, full_in.at[1, 1]))
        return waits

    def left_value(d, h):
        at = mod4(y + d) * 96 + 48 * h
        return pleft[rows_at(c * LOCAL + at, 48), :] + precv[rows_at(at, 48), :].astype(F32)

    waits = ring_sum(yp, ym, 96, left_value, cp, yrh, yrf, lambda: None)
    for wait in waits:
        wait()

    def left_rows(core, d, h=None):
        start = core * LOCAL + mod4(y + d) * 96
        if h is None:
            return left2.at[rows_at(start, 96)]
        return left2.at[rows_at(start + 48 * h, 48)]

    for h in range(2):
        total = left_value(0, h) + yrf[0, h].astype(F32) + yrf[1, h].astype(F32)
        left2[rows_at(c * LOCAL + y * 96 + 48 * h, 48), :] = total.astype(BF)
    mine = left_rows(c, 0)
    from_m = send(mine, mine, yp, left_rows(c, -1))
    from_p = send(mine, mine, ym, left_rows(c, 1))
    pair = [send(mine, mine, sib, left_rows(1 - c, 0))]
    from_m()
    ref = left_rows(c, -1, 0)
    opp0 = send(ref, ref, yp, left_rows(c, 2, 0))
    ref = left_rows(c, -1)
    pair.append(send(ref, ref, sib, left_rows(1 - c, -1)))
    from_p()
    ref = left_rows(c, 1, 1)
    opp1 = send(ref, ref, ym, left_rows(c, 2, 1))
    ref = left_rows(c, 1)
    pair.append(send(ref, ref, sib, left_rows(1 - c, 1)))
    opp0()
    opp1()
    ref = left_rows(c, 2)
    pair.append(send(ref, ref, sib, left_rows(1 - c, 2)))
    for wait in pair:
        wait()

    gs[...] = dotb(left2[:, rows_at(y * 128, 128, 128)], left2[...], ((0,), (0,)))

    def tile(base, j):
        return (
            rows_at(base + lax.div(j, 2) * 8, 8, 8),
            rows_at(lax.rem(j, 2) * 256, 256, 128),
        )

    j_me = x * 4 + z
    gram_in = []
    for e, (dx, dz) in enumerate(plane):
        rr, cc = tile(c * 64, mod4(x + dx) * 4 + mod4(z + dz))
        gram_in.append(send(gs.at[rr, cc], gr.at[e], peer(dx, dz), gr.at[e]))
    state = {}

    def gram_steps():
        for wait in gram_in:
            wait()
        rr, cc = tile(c * 64, j_me)
        total = gs[rr, cc]
        for e in range(15):
            total = total + gr[e]
        base = y * 128 + c * 64
        rr, cc = tile(base, j_me)
        gram[rr, cc] = total
        waits = []
        for dx, dz in plane:
            ref = gram.at[rr, cc]
            waits.append(
                send(ref, ref, peer(dx, dz), gram.at[tile(base, source_chip(dx, dz))])
            )
        state["gather"] = waits

    def z_value(d, h):
        at = rows_at(mod4(p1 + d) * SEG + (SEG // 2) * h, SEG // 2)
        return dotb(buf2t[at, :], left2[...], ((1,), (0,)))

    def gram_rows(core, d, h=None):
        start = mod4(y + d) * 128 + core * 64
        if h is None:
            return gram.at[rows_at(start, 64)]
        return gram.at[rows_at(start + 32 * h, 32)]

    def between():
        gram_steps()
        for h in range(2):
            zown[h] = z_value(0, h)
        for wait in state["gather"]:
            wait()
        mine = gram_rows(c, 0)
        state["m"] = send(mine, mine, yp, gram_rows(c, -1))
        state["p"] = send(mine, mine, ym, gram_rows(c, 1))
        state["pair"] = [send(mine, mine, sib, gram_rows(1 - c, 0))]

    z_waits = ring_sum(a1p, a1m, SEG, z_value, zp, zrh, zrf, between)
    state["m"]()
    ref = gram_rows(c, -1, 0)
    opp0 = send(ref, ref, yp, gram_rows(c, 2, 0))
    ref = gram_rows(c, -1)
    pair = state["pair"]
    pair.append(send(ref, ref, sib, gram_rows(1 - c, -1)))
    state["p"]()
    ref = gram_rows(c, 1, 1)
    opp1 = send(ref, ref, ym, gram_rows(c, 2, 1))
    ref = gram_rows(c, 1)
    pair.append(send(ref, ref, sib, gram_rows(1 - c, 1)))
    opp0()
    opp1()
    ref = gram_rows(c, 2)
    pair.append(send(ref, ref, sib, gram_rows(1 - c, 2)))
    for wait in pair:
        wait()
    tmat[...] = gram[...]

    def sub_rows(a, b):
        return rows_at(a * SEG + b * SUB, SUB)

    def sub_half(a, b, h):
        return rows_at(a * SEG + b * SUB + 112 * h, 112 - 16 * h)

    def to_sib(rows, landing):
        return plan(
            zfull.at[rows],
            zt_hbm.at[rows_at(c * HALF + rows.start, rows.size)],
            sib,
            zt_hbm.at[rows_at((1 - c) * HALF + landing.start, rows.size)],
        )

    def part(b):
        return zp.at[0, lax.div(b, 2), rows_at(lax.rem(b, 2) * SUB, SUB)]

    own = zfull.at[sub_rows(p1, p2)]
    z2, z3, z4, z5, zs = {}, {}, {}, {}, {}
    for d in (2, 1, 3):
        to = (device(p1, at2(d)), y)
        z2[d] = plan(part(at2(d)), zr2.at[d - 1], to, zr2.at[d - 1])
        z3[d] = plan(own, own, to, zfull.at[sub_rows(p1, at2(-d))])
    for d in range(4):
        b = at2(d)
        ref = zfull.at[sub_rows(p1, b)]
        z4[d] = (
            plan(ref, ref, a1p, zfull.at[sub_rows(at1(-1), b)]),
            plan(ref, ref, a1m, zfull.at[sub_rows(at1(1), b)]),
        )
        ref, ref1 = zfull.at[sub_half(at1(-1), b, 0)], zfull.at[sub_half(at1(1), b, 1)]
        z5[d] = (
            plan(ref, ref, a1p, zfull.at[sub_half(at1(2), b, 0)]),
            plan(ref1, ref1, a1m, zfull.at[sub_half(at1(2), b, 1)]),
        )
        for a in range(4):
            zs[a, d] = to_sib(sub_rows(at1(a), b), sub_rows(at2(a), at1(d)))

    def z_sum1():
        for wait in z_waits:
            wait()
        for h in range(2):

            def step(i, carry):
                at = rows_at(i * 16, 16)
                total = zown[h, at, :] + zrf[0, h, at, :].astype(F32)
                total = total + zrf[1, h, at, :].astype(F32)
                zp[0, h, at, :] = total.astype(BF)
                return carry

            lax.fori_loop(0, SEG // 32, step, 0)
        for start, _ in z2.values():
            start()

    def z_out(d):
        z4[d][0][0]()
        z4[d][1][0]()
        zs[0, d][0]()

    def z_sum2():
        for _, wait in z2.values():
            wait()

        def step(i, carry):
            at = rows_at(i * 16, 16)
            mine = rows_at(lax.rem(p2, 2) * SUB + i * 16, 16)
            total = zp[0, lax.div(p2, 2), mine, :].astype(F32)
            for d in range(3):
                total = total + zr2[d, at, :].astype(F32)
            zfull[rows_at(p1 * SEG + p2 * SUB + i * 16, 16), :] = total.astype(BF)
            return carry

        lax.fori_loop(0, SUB // 16, step, 0)
        for start, _ in z3.values():
            start()
        z_out(0)

    def z_gather2(d):
        z3[d][1]()
        z_out((4 - d) % 4)

    def z_forward(d):
        (_, from_m), (_, from_p) = z4[d]
        from_m()
        z5[d][0][0]()
        zs[3, d][0]()
        from_p()
        z5[d][1][0]()
        zs[1, d][0]()

    def z_last(d):
        for _, wait in z5[d]:
            wait()
        zs[2, d][0]()

    steps = {
        (0, 3): z_sum1,
        (2, 0): z_sum2,
        (3, 1): lambda: z_gather2(1),
        (3, 2): lambda: z_gather2(3),
        (3, 3): lambda: z_gather2(2),
    }

    def hook(k, part):
        for (at, which), step in steps.items():
            if which == part:
                pl.when(k == at)(step)

    chol_inv(tmat, wmat, hook)
    ri = lax.broadcasted_iota(jnp.int32, (RANK, RANK), 0)
    ci = lax.broadcasted_iota(jnp.int32, (RANK, RANK), 1)
    tmat[...] = jnp.where(ci <= ri, tmat[...], 0.0)
    w_hi, w_lo = split(tmat[...])

    shard = zfull[sub_rows(p1, p2), :]
    right = dotb(shard, w_hi, ((1,), (1,))) + dotb(shard, w_lo, ((1,), (1,)))
    nr1[0] = jnp.sum((right * right).reshape(SUB // 8, 8, RANK), axis=0)
    norm_in = [
        send(nr1.at[0], nr1.at[e + 1], peer(dx, dz), nr1.at[e + 1])
        for e, (dx, dz) in enumerate(plane)
    ]
    z_forward(0)
    own_left = left2[my_rows, :]
    ortho = (dotb(own_left, w_hi, ((1,), (1,))) + dotb(own_left, w_lo, ((1,), (1,)))).astype(BF)
    lhs_ref[0:LOCAL, :] = (
        dotb(ortho, w_hi, ((1,), (0,))) + dotb(ortho, w_lo, ((1,), (0,)))
    ).astype(BF)
    for wait in norm_in:
        wait()
    total = nr1[0]
    for e in range(15):
        total = total + nr1[e + 1]
    nr2[0] = total
    norm_in = [
        send(nr2.at[0], nr2.at[f + 1], member(dy, dc), nr2.at[f + 1])
        for f, (dy, dc) in enumerate(group)
    ]
    z_forward(3)
    z_forward(1)
    for wait in norm_in:
        wait()
    total = nr2[0]
    for f in range(7):
        total = total + nr2[f + 1]
    scale = lax.rsqrt(jnp.sum(total, axis=0, keepdims=True) + 1e-06)
    sub16 = lax.broadcasted_iota(jnp.int32, (16, RANK), 0)
    lane16 = lax.broadcasted_iota(jnp.int32, (16, RANK), 1)
    pick = jnp.where(lane16 == sub16 + r * 16, scale, 0.0)
    o_hi, o_lo = split(jnp.concatenate([ortho.astype(F32) * scale, pick], axis=0))
    lhs_ref[LOCAL : 2 * LOCAL + 16, :] = (
        dotb(o_hi, w_hi, ((1,), (0,)))
        + (dotb(o_hi, w_lo, ((1,), (0,))) + dotb(o_lo, w_hi, ((1,), (0,))))
    ).astype(BF)
    z_forward(2)
    for d in (0, 3, 1, 2):
        z_last(d)
    out = pltpu.make_async_copy(zfull, zt_hbm.at[rows_at(c * HALF, HALF)], load_sem.at[10])
    out.start()
    for _, wait in zs.values():
        wait()
    out.wait()
    for wait in sent:
        wait()


def gather_call(momentum, gradient, basis):
    anyspace = pl.BlockSpec(memory_space=pl.ANY)
    vmem = pl.BlockSpec(memory_space=pltpu.VMEM)
    scratch = [
        ((2, LOCAL, PART), BF),
        ((2, LOCAL, PART), BF),
        ((LOCAL, HALF), BF),
        ((2 * LOCAL, HALF), BF),
        ((HALF, 2 * LOCAL), BF),
        ((RANK, HALF), BF),
        ((2 * LOCAL, RANK), F32),
        ((LOCAL, RANK), BF),
        ((LOCAL, RANK), BF),
        ((4, 2, 48, RANK), BF),
        ((2, 48, RANK), BF),
        ((2, 2, 48, RANK), BF),
        ((2 * LOCAL, RANK), BF),
        ((128, RANK), F32),
        ((15, 8, 256), F32),
        ((RANK, RANK), F32),
        ((RANK, RANK), F32),
        ((B, B), F32),
        ((4, 2, SEG // 2, RANK), BF),
        ((2, SEG // 2, RANK), F32),
        ((2, SEG // 2, RANK), BF),
        ((2, 2, SEG // 2, RANK), BF),
        ((3, SUB, RANK), BF),
        ((HALF, RANK), BF),
        ((16, 8, RANK), F32),
        ((8, 8, RANK), F32),
    ]
    return pl.pallas_call(
        gather_kernel,
        out_shape=(
            jax.ShapeDtypeStruct((COLS, RANK), BF),
            jax.ShapeDtypeStruct((2 * LOCAL + 16, RANK), BF),
        ),
        in_specs=[anyspace] * 3,
        out_specs=(anyspace, vmem),
        scratch_shapes=[pltpu.VMEM(s, t) for s, t in scratch]
        + [
            pltpu.SemaphoreType.DMA((11,)),
            pltpu.SemaphoreType.DMA((N_SEMS,)),
            pltpu.SemaphoreType.DMA((N_SEMS,)),
        ],
        compiler_params=pltpu.CompilerParams(
            collective_id=0, has_side_effects=True, vmem_limit_bytes=56 << 20
        ),
        name="project",
    )(momentum, gradient, basis)


def apply_kernel(m_ref, g_ref, zt_ref, lhs_ref, mom_ref, bas_ref, upd_ref):
    prod = dotb(lhs_ref[...], zt_ref[...], ((1,), (1,)))
    total = (m_ref[...].astype(F32) + g_ref[...].astype(F32)).astype(BF).astype(F32)
    mom_ref[...] = (total - 0.2 * prod[:LOCAL]).astype(BF)
    factor = math.sqrt(ROWS * WIDTH / RANK)
    upd_ref[...] = (factor * prod[LOCAL : 2 * LOCAL]).astype(BF)
    bas_ref[...] = prod[2 * LOCAL :].astype(BF)


def apply_call(momentum, gradient, zt, lhs):
    wide = 512
    block = pl.BlockSpec((LOCAL, wide), lambda i: (0, i))
    return pl.pallas_call(
        apply_kernel,
        grid=(COLS // wide,),
        out_shape=(
            jax.ShapeDtypeStruct((LOCAL, COLS), BF),
            jax.ShapeDtypeStruct((16, COLS), BF),
            jax.ShapeDtypeStruct((LOCAL, COLS), BF),
        ),
        in_specs=[
            block,
            block,
            pl.BlockSpec((wide, RANK), lambda i: (i, 0)),
            pl.BlockSpec((2 * LOCAL + 16, RANK), lambda i: (0, 0)),
        ],
        out_specs=(block, pl.BlockSpec((16, wide), lambda i: (0, i)), block),
        compiler_params=pltpu.CompilerParams(vmem_limit_bytes=40 << 20),
        name="apply",
    )(momentum, gradient, zt, lhs)


def local(momentum, gradient, basis):
    zt, lhs = gather_call(momentum, gradient, basis)
    return apply_call(momentum, gradient, zt, lhs)


def solution(mesh):
    return jax.shard_map(
        local,
        mesh=mesh,
        in_specs=(P("rows", "cols"), P("rows", "cols"), P("rows", "cols")),
        out_specs=(P("rows", "cols"), P("rows", "cols"), P("rows", "cols")),
        check_vma=False,
    )
```

time: 532 us -> 145 us (0.27)
  waiting for transfers between devices: 319 us -> 0 us
  Pallas kernels: 0 us -> 140 us
  other arithmetic: 130 us -> 0 us
  matrix products: 41.5 us -> 0 us
  between operations: 16.8 us -> 0.66 us
  blocking collectives: 8.69 us -> 0 us
  local copies, waits for them, and re-layouts: 10 us -> 3.59 us
    psum x3 -> x0, waiting for transfers between devices: 262 us -> none  [the longest x1 117 us: local(): right = lax.psum(local_right.astype(jnp.bfloat16), 'rows')]
    pallas_call x0 -> x2, Pallas kernels: none -> 140 us  [the longest x1 127 us: gather_call(): pl.pallas_call(gather_kernel, out_shape=(jax.ShapeDtypeStruct((COLS, RANK...]
    another operation x17 -> x0, other arithmetic: 118 us -> none  [the longest x14 78.5 us: local(): lower = jnp.linalg.cholesky(gram)]
    all_gather x1 -> x0, waiting for transfers between devices: 56.1 us -> none  [local(): lax.all_gather(basis, 'rows', axis=0, tiled=True)]
    dot_general x5 -> x0, matrix products: 34.9 us -> none  [the longest x1 10.5 us: local(): lax.dot_general(ortho, buffer, (((0,), (0,)), ((), ())), preferred_elemen...]
    psum x1 -> x0, blocking collectives: 8.69 us -> none  [local(): squares = lax.psum(jnp.sum(right_wide * right_wide, axis=1), 'cols')]
    another operation x17 -> x0, local copies, waits for them, and re-layouts: 8.07 us -> none
    another operation x13 -> x0, matrix products: 6.69 us -> none  [the longest x7 4.82 us: local(): jax.scipy.linalg.solve_triangular(lower, left.T, lower=True)]
  transfers between devices with their start and end apart: 4 -> 0, of which waited for: 4 -> 0; matrix products, arithmetic and copies ran while one was open for 0% -> 0% of each run, Pallas kernels for 0% -> 0%
where the time goes in v1:
time: 145 us
  Pallas kernels  140 us (97%)
  local copies, waits for them, and re-layouts  3.59 us (2%)
    pallas_call x1, Pallas kernels, gather_call(): pl.pallas_call(gather_kernel, out_shape=(jax.ShapeDtypeStruct((COLS, RANK...  127 us
    pallas_call x1, Pallas kernels, apply_call(): pl.pallas_call(apply_kernel, grid=(COLS // wide,), out_shape=(jax.ShapeDt...  13.8 us
    unnamed x6, local copies, waits for them, and re-layouts  3.59 us

profile of v1, /device:TPU:1, one launch (start us, length us, event | category | flops | bytes accessed | tf_op | source)
XLA Modules:
  0.0 144.7 jit_solution(12850675620124846273)
XLA Ops:
  0.6 0.0 copy-start
  0.6 126.6 %project.1 = (bf16[6656,512]{1,0:T(8,128)(2,1)}, bf16[784,512]{1,0:T(8,128)(2,1)}) custom-call(bf16[384,6656]{1,0:T(8,128)(2,1)} %m_ref.1, bf16[384,6656]{1,0:T(8,128)(2,1)} %g_ref.1, bf16[16,6656]{1,0:T(8,128)(2,1)} %basis_hbm.1), custom_call_target="tpu_custom_call" | custom-call | tf_op jit(solution)/shard_map/project/pallas_call | solution.py:680
  127.2 0.0 copy-done
  127.2 0.0 copy-start.1
  127.2 2.4 %copy-done.1 = bf16[384,6656]{1,0:T(8,128)(2,1)S(1)} copy-done((bf16[384,6656]{1,0:T(8,128)(2,1)S(1)}, bf16[384,6656]{1,0:T(8,128)(2,1)}, u32[]{:S(2)}) %copy-start.1) | copy-done | bytes 5111832
  129.7 0.0 copy-start.2
  129.7 1.1 copy-done.2
  130.8 13.8 %apply.1 = (bf16[384,6656]{1,0:T(8,128)(2,1)}, bf16[16,6656]{1,0:T(8,128)(2,1)}, bf16[384,6656]{1,0:T(8,128)(2,1)}) custom-call(bf16[384,6656]{1,0:T(8,128)(2,1)S(1)} %copy-done, bf16[384,6656]{1,0:T(8,128)(2,1)S(1)} %copy-done.1, bf16[6656,512]{1,0:T(8,128)(2,1)} %get-tuple-element.5.zt_ref, bf16[784,512]{1,0:T(8,128)(2,1)S(1)} %copy-done.2), custom_call_target="tpu_custom_call" | custom-call | tf_op jit(solution)/shard_map/apply/pallas_call | solution.py:713
Async XLA Ops:
  0.6 126.6 %copy-start = (bf16[384,6656]{1,0:T(8,128)(2,1)S(1)}, bf16[384,6656]{1,0:T(8,128)(2,1)}, u32[]{:S(2)}) copy-start(bf16[384,6656]{1,0:T(8,128)(2,1)} %m_ref.1) | copy-start | bytes 15335428
  127.2 2.5 %copy-start.1 = (bf16[384,6656]{1,0:T(8,128)(2,1)S(1)}, bf16[384,6656]{1,0:T(8,128)(2,1)}, u32[]{:S(2)}) copy-start(bf16[384,6656]{1,0:T(8,128)(2,1)} %g_ref.1) | copy-start | bytes 15335428
  129.7 1.1 copy-start.2

commit v2 on v1

v2 whole, which is shorter than its diff:
```python
import functools
import math

import jax
import jax.numpy as jnp
from jax import lax
from jax.experimental import pallas as pl
from jax.experimental.pallas import tpu as pltpu
from jax.sharding import PartitionSpec as P

ROWS = 12288
WIDTH = 26624
RANK = 512
MESH = pl.DeviceIdType.MESH
BF = jnp.bfloat16
F32 = jnp.float32

LOCAL = 384
COLS = 6656
HALF = 3328
PART = 1664
SEG = 832
SUB = 208
B = 128
N_SEMS = 224


def mod4(v):
    return lax.rem(v + 4, 4)


def rows_at(start, size, unit=16):
    return pl.ds(pl.multiple_of(start, unit), size)


def dotp(a, b, dims):
    return lax.dot_general(
        a, b, (dims, ((), ())), precision=lax.Precision.HIGHEST, preferred_element_type=F32
    )


def dotb(a, b, dims):
    return lax.dot_general(a, b, (dims, ((), ())), preferred_element_type=F32)


def split(a):
    hi = a.astype(BF)
    return hi, (a - hi.astype(F32)).astype(BF)


def tree(terms):
    while len(terms) > 1:
        terms = [a + b for a, b in zip(terms[::2], terms[1::2])]
    return terms[0]


def sweep(w_ref, t, hook):
    sub = lax.broadcasted_iota(jnp.int32, (8, B), 0)
    lane = lax.broadcasted_iota(jnp.int32, (8, B), 1)
    panels = B // 8
    for p in range(panels):
        top = t[:8]
        cols = jnp.stack(
            [jnp.broadcast_to(top[:, 8 * p + j : 8 * p + j + 1], (8, B)) for j in range(8)]
        )
        for j in range(0, 8, 2):
            d0 = jnp.broadcast_to(cols[j, j : j + 1, :], (8, B))
            off = jnp.broadcast_to(cols[j, j + 1 : j + 2, :], (8, B))
            d1 = jnp.broadcast_to(cols[j + 1, j + 1 : j + 2, :], (8, B))
            r0 = lax.rsqrt(d0)
            r1 = lax.rsqrt(d0 * d1 - off * off) * (d0 * r0)
            low = off * r0
            below = sub > j + 1
            m0 = jnp.where(below, cols[j] * r0, 0.0)
            m1 = jnp.where(below, (cols[j + 1] - m0 * low) * r1, 0.0)
            c0 = jnp.where(sub >= j, jnp.where(sub == j, 1.0, 0.0), cols[j])
            c1 = jnp.where(sub >= j, jnp.where(sub == j + 1, 1.0, 0.0), cols[j + 1])
            parts = [cols[:j]] if j else []
            parts += [c0[None], c1[None]]
            if j < 6:
                parts.append(cols[j + 2 :])
            cols = jnp.concatenate(parts, axis=0)
            s0 = cols[:, j : j + 1, :] * r0[None]
            s1 = (cols[:, j + 1 : j + 2, :] - low[None] * s0) * r1[None]
            rest = cols - m0[None] * s0 - m1[None] * s1
            cols = jnp.where((sub == j)[None], s0, jnp.where((sub == j + 1)[None], s1, rest))
        tri = [jnp.where(sub >= k, cols[k], 0.0) for k in range(8)]
        inside = (lane >= 8 * p) & (lane < 8 * p + 8)
        eye = jnp.where(inside, jnp.where(lane - 8 * p == sub, 1.0, 0.0), top)
        new = tree([tri[k] * eye[k : k + 1] for k in range(8)])
        w_ref[8 * p : 8 * p + 8, :] = jnp.where(lane <= sub + 8 * p, new, 0.0)
        if p < panels - 1:
            rest = t[8:]
            lanes = lax.broadcasted_iota(jnp.int32, rest.shape, 1)
            t = jnp.where((lanes >= 8 * p) & (lanes < 8 * p + 8), 0.0, rest)
            ys = [jnp.sum(tri[k] * new, axis=0, keepdims=True) for k in range(8)]
            t = t - tree([rest[:, 8 * p + k : 8 * p + k + 1] * ys[k] for k in range(8)])
        if p % 2 == 1:
            hook(p // 2)


def chol_inv(t_ref, w_ref, hook):
    lanes = lax.broadcasted_iota(jnp.int32, (B, RANK), 1)
    subs = lax.broadcasted_iota(jnp.int32, (B, RANK), 0)

    def block(k, carry):
        base = pl.multiple_of(k * B, B)
        rows = pl.ds(base, B)
        sweep(w_ref, t_ref[rows, rows], functools.partial(hook, k))
        own = (lanes >= base) & (lanes < base + B)
        mine = jnp.where(own, jnp.where(lanes - base == subs, 1.0, 0.0), t_ref[rows, :])
        new = dotp(w_ref[...], mine, ((1,), (0,)))
        t_ref[rows, :] = new

        def below(i, c):
            at = pl.ds(pl.multiple_of(i * B, B), B)
            t_ref[at, :] = jnp.where(own, 0.0, t_ref[at, :]) - dotp(
                t_ref[rows, at], new, ((0,), (0,))
            )
            return c

        lax.fori_loop(k + 1, RANK // B, below, 0)
        return carry

    lax.fori_loop(0, RANK // B, block, 0)


def gather_kernel(
    m_hbm, g_hbm, basis_hbm, buf_ref, zt_ref, lhs_ref,
    mbuf, gbuf, side, buf2t, bas, psum, pleft, psend, precv, chip_left, yr, left2,
    gs, gr, gram, tmat, wmat, zp, zown, zl, zrh, zrf, zr2, nr1, nr2,
    load_sem, send_sem, recv_sem,
):
    r = lax.axis_index("rows")
    y = lax.axis_index("cols")
    c = lax.rem(r, 2)
    z = lax.rem(lax.div(r, 2), 4)
    x = lax.div(r, 8)
    p1 = x * (1 - c) + z * c
    p2 = z * (1 - c) + x * c

    def chip(a, b):
        return a * (4 - 3 * c) + b * (1 + 3 * c)

    def device(a, b):
        return 2 * chip(a, b) + c

    sib = (r + 1 - 2 * c, y)
    a1p = (device(mod4(p1 + 1), p2), y)
    a1m = (device(mod4(p1 - 1), p2), y)
    a2p = (device(p1, mod4(p2 + 1)), y)
    a2m = (device(p1, mod4(p2 - 1)), y)
    plane = [(dx, dz) for dx in range(4) for dz in range(4) if dx or dz]

    def peer(dx, dz):
        return (mod4(x + dx) * 8 + mod4(z + dz) * 2 + c, y)

    def source_chip(dx, dz):
        return mod4(x - dx) * 4 + mod4(z - dz)

    group = [(dy, dc) for dy in range(4) for dc in range(2) if dy or dc]

    def member(dy, dc):
        return (r + dc * (1 - 2 * c), mod4(y + dy))

    count = [0]
    sent = []

    def plan(src, dst, to, landing):
        i = count[0]
        count[0] += 1

        def copy(s, d):
            return pltpu.make_async_remote_copy(
                s, d, send_sem.at[i], recv_sem.at[i], device_id=to, device_id_type=MESH
            )

        def start():
            copy(src, dst).start()
            sent.append(lambda: copy(src, dst).wait_send())

        return start, lambda: copy(landing, landing).wait_recv()

    def send(src, dst, to, landing):
        start, wait = plan(src, dst, to, landing)
        start()
        return wait

    def columns(core, part):
        return pl.ds(pl.multiple_of(core * HALF + part * PART, 128), PART)

    order = [(1 - c, 0), (1 - c, 1), (c, 0), (c, 1)]

    def load(n):
        at = columns(*order[n])
        return [
            pltpu.make_async_copy(m_hbm.at[:, at], mbuf.at[n % 2], load_sem.at[2 * n]),
            pltpu.make_async_copy(g_hbm.at[:, at], gbuf.at[n % 2], load_sem.at[2 * n + 1]),
        ]

    loads = [load(n) for n in range(4)]
    for n in range(2):
        for copy in loads[n]:
            copy.start()
    own_rows = rows_at(r * 16, 16)
    parts = [pl.ds(0, PART), pl.ds(PART, PART)]
    own_basis = [
        pltpu.make_async_copy(
            basis_hbm.at[:, columns(c, n)], bas.at[own_rows, parts[n]], load_sem.at[8 + n]
        )
        for n in range(2)
    ]
    for copy in own_basis:
        copy.start()

    barrier = pltpu.get_barrier_semaphore()
    others = [sib, a1p, a1m, a2p, a2m] + [(r, mod4(y + d)) for d in (1, 2, 3)]
    for to in others:
        pl.semaphore_signal(barrier, inc=1, device_id=to, device_id_type=MESH)
    pl.semaphore_wait(barrier, len(others))

    sib_ranks = rows_at((r + 1 - 2 * c) * 16, 16)
    got = [
        send(
            basis_hbm.at[:, columns(1 - c, n)],
            bas.at[own_rows, parts[n]],
            sib,
            bas.at[sib_ranks, parts[n]],
        )
        for n in range(2)
    ]

    def piece(a, b, n):
        return bas.at[rows_at(chip(a, b) * 32, 32), parts[n]]

    def half_piece(a, b, n, h):
        return bas.at[rows_at(chip(a, b) * 32 + 16 * h, 16), parts[n]]

    def at1(d):
        return mod4(p1 + d)

    def at2(d):
        return mod4(p2 + d)

    first = []
    for n in range(2):
        own_basis[n].wait()
        got[n]()
        mine = piece(p1, p2, n)
        first.append(
            (
                send(mine, mine, a1p, piece(at1(-1), p2, n)),
                send(mine, mine, a1m, piece(at1(1), p2, n)),
            )
        )

    def both2(a, n):
        ref = piece(a, p2, n)
        return (
            send(ref, ref, a2p, piece(a, at2(-1), n)),
            send(ref, ref, a2m, piece(a, at2(1), n)),
        )

    second = [[both2(p1, n)] for n in range(2)]

    def add_loaded(n):
        for copy in loads[n]:
            copy.wait()

        def step(i, carry):
            at = rows_at(i * 16, 16)
            total = mbuf[n % 2, at, :].astype(F32) + gbuf[n % 2, at, :].astype(F32)
            buf_ref[at, columns(*order[n])] = total.astype(BF)
            return carry

        lax.fori_loop(0, LOCAL // 16, step, 0)
        if n < 2:
            for copy in loads[n + 2]:
                copy.start()

    my_rows = rows_at(c * LOCAL, LOCAL, 128)
    sib_rows = rows_at((1 - c) * LOCAL, LOCAL, 128)

    def send_buffer(n):
        return send(
            buf_ref.at[:, columns(1 - c, n)], side.at[:, parts[n]], sib, side.at[:, parts[n]]
        )

    def turn(n, mine):
        def step(i, carry):
            at = rows_at(n * PART + i * 128, 128, 128)
            if mine:
                from_at = rows_at(c * HALF + n * PART + i * 128, 128, 128)
                buf2t[at, my_rows] = buf_ref[:, from_at].T
            else:
                buf2t[at, sib_rows] = side[:, at].T
            return carry

        lax.fori_loop(0, PART // 128, step, 0)

    add_loaded(0)
    swapped = [send_buffer(0)]
    opposite1 = []
    for n in range(2):
        from_m, from_p = first[n]
        from_m()
        ref = half_piece(at1(-1), p2, n, 0)
        opp0 = send(ref, ref, a1p, half_piece(at1(2), p2, n, 0))
        second[n].append(both2(at1(-1), n))
        from_p()
        ref = half_piece(at1(1), p2, n, 1)
        opp1 = send(ref, ref, a1m, half_piece(at1(2), p2, n, 1))
        second[n].append(both2(at1(1), n))
        opposite1.append((opp0, opp1))
    add_loaded(1)
    swapped.append(send_buffer(1))
    for n in range(2):
        for wait in opposite1[n]:
            wait()
        second[n].append(both2(at1(2), n))
    add_loaded(2)
    last = [[], []]
    offsets = (0, -1, 1, 2)

    def forward2(n, q):
        a = at1(offsets[q])
        from_m, from_p = second[n][q]
        from_m()
        ref = half_piece(a, at2(-1), n, 0)
        last[n].append(send(ref, ref, a2p, half_piece(a, at2(2), n, 0)))
        from_p()
        ref = half_piece(a, at2(1), n, 1)
        last[n].append(send(ref, ref, a2m, half_piece(a, at2(2), n, 1)))

    forward2(0, 0)
    forward2(0, 1)
    add_loaded(3)
    forward2(0, 2)
    forward2(0, 3)
    forward2(1, 0)
    turn(0, True)
    forward2(1, 1)
    turn(1, True)
    swapped[0]()
    turn(0, False)
    forward2(1, 2)
    swapped[1]()
    turn(1, False)
    forward2(1, 3)

    ranks = [pl.ds(0, 256), pl.ds(256, 256)]

    def left_part(mine, n, s):
        rows = buf_ref[:, columns(c, n)] if mine else side[:, parts[n]]
        return dotb(rows, bas[ranks[s], parts[n]], ((1,), (1,)))

    for wait in last[0]:
        wait()
    for s in range(2):
        psum[s] = left_part(False, 0, s)
        pleft[s] = left_part(True, 0, s)
    for wait in last[1]:
        wait()
    paired = []
    for s in range(2):
        psend[s] = (psum[s] + left_part(False, 1, s)).astype(BF)
        paired.append(send(psend.at[s], precv.at[s], sib, precv.at[s]))
        pleft[s] = pleft[s] + left_part(True, 1, s)

    def along_y(d):
        return (r, mod4(y + d))

    def left_rows(core, d):
        return rows_at(core * LOCAL + mod4(y + d) * 96, 96)

    summed = []
    for s in range(2):
        paired[s]()
        total = pleft[s] + precv[s].astype(F32)
        pleft[s] = total
        chip_left[s] = total.astype(BF)
        summed.append(
            [
                send(
                    chip_left.at[s, rows_at(mod4(y + d) * 96, 96)],
                    yr.at[s, d - 1],
                    along_y(d),
                    yr.at[s, d - 1],
                )
                for d in (2, 1, 3)
            ]
        )
    spread, pairs = [], []
    for s in range(2):
        for wait in summed[s]:
            wait()
        total = pleft[s, rows_at(y * 96, 96), :]
        for d in range(3):
            total = total + yr[s, d].astype(F32)
        left2[s, left_rows(c, 0), :] = total.astype(BF)
        ref = left2.at[s, left_rows(c, 0)]
        spread.append(
            {d: send(ref, ref, along_y(d), left2.at[s, left_rows(c, -d)]) for d in (2, 1, 3)}
        )
        pairs.append([send(ref, ref, sib, left2.at[s, left_rows(1 - c, 0)])])

    def left_done(s):
        for d in (1, 3, 2):
            spread[s][d]()
            ref = left2.at[s, left_rows(c, -d)]
            pairs[s].append(send(ref, ref, sib, left2.at[s, left_rows(1 - c, -d)]))
        for wait in pairs[s]:
            wait()

    def z_value(d, h, s):
        at = rows_at(mod4(p1 + d) * SEG + (SEG // 2) * h, SEG // 2)
        return dotb(buf2t[at, :], left2[s], ((1,), (0,)))

    ways = (a1p, a1m)
    z_half = [[], []]
    z_full = [[], []]

    def z_first(s):
        for w in range(2):
            zp[s, 2, w] = z_value(2, w, s).astype(BF)
            z_half[s].append(send(zp.at[s, 2, w], zrh.at[s, w], ways[w], zrh.at[s, w]))

    def z_middle(s):
        for w, (d, h) in enumerate(((1, 1), (3, 0))):
            zp[s, d, h] = z_value(d, h, s).astype(BF)
            z_full[s].append(send(zp.at[s, d, h], zrf.at[s, w, h], ways[w], zrf.at[s, w, h]))

    def z_prepare(s):
        for w, (d, h) in enumerate(((1, 0), (3, 1))):
            zl[s, w] = z_value(d, h, s)

    def z_add(s):
        for w, (d, h) in enumerate(((1, 0), (3, 1))):
            z_half[s][w]()
            zp[s, d, h] = (zl[s, w] + zrh[s, w].astype(F32)).astype(BF)
            z_full[s].append(send(zp.at[s, d, h], zrf.at[s, w, h], ways[w], zrf.at[s, w, h]))

    def z_own(s):
        for h in range(2):
            zown[s, h] = z_value(0, h, s)

    left_done(0)
    z_first(0)
    left_done(1)

    blocks = [(i, j) for i in range(4) for j in range(i, 4)]

    def left_block(i):
        return left2[i // 2, :, 128 * (i % 2) : 128 * (i % 2) + 128]

    for b, (i, j) in enumerate(blocks):
        gs[b] = dotb(left_block(i), left_block(j), ((0,), (0,)))

    def tile(j):
        return pl.ds(lax.rem(j, 2) * 5, 5), rows_at(c * 64 + lax.div(j, 2) * 8, 8, 8)

    gram_in = []
    for e, (dx, dz) in enumerate(plane):
        to = tile(mod4(x + dx) * 4 + mod4(z + dz))
        gram_in.append(send(gs.at[to], gr.at[e], peer(dx, dz), gr.at[e]))
    z_first(1)
    z_middle(0)
    for wait in gram_in:
        wait()
    mine = tile(x * 4 + z)
    gram[mine] = gs[mine] + tree([gr[e] for e in range(15)] + [jnp.zeros((5, 8, B), F32)])
    gathered = []
    for dx, dz in plane:
        ref = gram.at[mine]
        gathered.append(send(ref, ref, peer(dx, dz), gram.at[tile(source_chip(dx, dz))]))
    z_middle(1)
    z_prepare(0)
    z_add(0)
    z_prepare(1)
    z_add(1)
    z_own(0)
    z_own(1)
    for wait in gathered:
        wait()
    ref = gram.at[:, rows_at(c * 64, 64)]
    send(ref, ref, sib, gram.at[:, rows_at((1 - c) * 64, 64)])()

    on = lax.broadcasted_iota(jnp.int32, (B, B), 0) == lax.broadcasted_iota(jnp.int32, (B, B), 1)
    across, down = [], []
    for i in range(4):
        diag = jnp.where(on, gram[blocks.index((i, i))], 0.0)
        across.append(lax.rsqrt(jnp.sum(diag, axis=0, keepdims=True)))
        down.append(lax.rsqrt(jnp.sum(diag, axis=1, keepdims=True)))
    for i in range(4):
        for j in range(4):
            if j < i:
                block = jnp.zeros((B, B), F32)
            else:
                block = gram[blocks.index((i, j))] * down[i] * across[j]
            tmat[B * i : B * i + B, B * j : B * j + B] = block

    def sub_rows(a, b):
        return rows_at(c * HALF + a * SEG + b * SUB, SUB)

    def sub_half(a, b, h):
        return rows_at(c * HALF + a * SEG + b * SUB + 112 * h, 112 - 16 * h)

    def to_sib(a, d, s):
        ref = zt_ref.at[sub_rows(at1(a), at2(d)), ranks[s]]
        start = (1 - c) * HALF + at2(a) * SEG + at1(d) * SUB
        return plan(ref, ref, sib, zt_ref.at[rows_at(start, SUB), ranks[s]])

    def part(b, s):
        return zp.at[s, 0, lax.div(b, 2), rows_at(lax.rem(b, 2) * SUB, SUB)]

    z2, z3, z4, z5, zs = {}, {}, {}, {}, {}
    for s in range(2):

        def sub(a, b, s=s):
            return zt_ref.at[sub_rows(a, b), ranks[s]]

        def half(a, b, h, s=s):
            return zt_ref.at[sub_half(a, b, h), ranks[s]]

        own = sub(p1, p2)
        for d in (2, 1, 3):
            to = (device(p1, at2(d)), y)
            z2[s, d] = plan(part(at2(d), s), zr2.at[s, d - 1], to, zr2.at[s, d - 1])
            z3[s, d] = plan(own, own, to, sub(p1, at2(-d)))
        for d in range(4):
            b = at2(d)
            ref = sub(p1, b)
            z4[s, d] = (
                plan(ref, ref, a1p, sub(at1(-1), b)),
                plan(ref, ref, a1m, sub(at1(1), b)),
            )
            ref, ref1 = half(at1(-1), b, 0), half(at1(1), b, 1)
            z5[s, d] = (
                plan(ref, ref, a1p, half(at1(2), b, 0)),
                plan(ref1, ref1, a1m, half(at1(2), b, 1)),
            )
            for a in range(4):
                zs[s, a, d] = to_sib(a, d, s)

    def z_sum1(s):
        for wait in z_full[s]:
            wait()

        def step(i, carry):
            h, at = lax.div(i, 2), rows_at(lax.rem(i, 2) * SUB, SUB)
            total = zown[s, h, at, :] + zrf[s, 0, h, at, :].astype(F32)
            total = total + zrf[s, 1, h, at, :].astype(F32)
            zp[s, 0, h, at, :] = total.astype(BF)
            return carry

        lax.fori_loop(0, 4, step, 0)
        for d in (2, 1, 3):
            z2[s, d][0]()

    def z_out(d, s):
        z4[s, d][0][0]()
        z4[s, d][1][0]()
        zs[s, 0, d][0]()

    def z_sum2(s):
        for d in (1, 3, 2):
            z2[s, d][1]()
        total = zp[s, 0, lax.div(p2, 2), rows_at(lax.rem(p2, 2) * SUB, SUB), :].astype(F32)
        for d in range(3):
            total = total + zr2[s, d].astype(F32)
        zt_ref[sub_rows(p1, p2), ranks[s]] = total.astype(BF)
        for d in (2, 1, 3):
            z3[s, d][0]()
        z_out(0, s)

    def z_gather2(d, s):
        z3[s, d][1]()
        z_out((4 - d) % 4, s)

    def z_forward(d, s):
        (_, from_m), (_, from_p) = z4[s, d]
        from_m()
        z5[s, d][0][0]()
        zs[s, 3, d][0]()
        from_p()
        z5[s, d][1][0]()
        zs[s, 1, d][0]()

    def z_last(d, s):
        for _, wait in z5[s, d]:
            wait()
        zs[s, 2, d][0]()

    steps = {
        (0, 5): lambda: z_sum1(0),
        (1, 1): lambda: z_sum1(1),
        (2, 0): lambda: z_sum2(0),
        (2, 6): lambda: z_sum2(1),
        (3, 0): lambda: z_forward(0, 0),
        (3, 2): lambda: z_gather2(1, 0),
        (3, 3): lambda: z_gather2(3, 0),
        (3, 4): lambda: z_gather2(2, 0),
        (3, 5): lambda: z_forward(0, 1),
        (3, 7): lambda: z_gather2(1, 1),
    }

    def hook(k, part):
        for (at, which), step in steps.items():
            if which == part:
                pl.when(k == at)(step)

    chol_inv(tmat, wmat, hook)
    ri = lax.broadcasted_iota(jnp.int32, (RANK, RANK), 0)
    ci = lax.broadcasted_iota(jnp.int32, (RANK, RANK), 1)
    tmat[...] = jnp.where(ci <= ri, tmat[...], 0.0) * jnp.concatenate(across, axis=1)
    w_hi, w_lo = split(tmat[...])

    shard = zt_ref[sub_rows(p1, p2), :]
    right = dotb(shard, w_hi, ((1,), (1,))) + dotb(shard, w_lo, ((1,), (1,)))
    squares = jnp.sum(right * right, axis=0, keepdims=True)
    rows = [squares[:, B * i : B * i + B] for i in range(4)] + [jnp.zeros((4, B), F32)]
    nr1[0] = jnp.concatenate(rows, axis=0)
    norm_in = [
        send(nr1.at[0], nr1.at[e + 1], peer(dx, dz), nr1.at[e + 1])
        for e, (dx, dz) in enumerate(plane)
    ]
    z_gather2(3, 1)
    z_gather2(2, 1)
    own_left = jnp.concatenate([left2[0, my_rows, :], left2[1, my_rows, :]], axis=1)
    ortho = (dotb(own_left, w_hi, ((1,), (1,))) + dotb(own_left, w_lo, ((1,), (1,)))).astype(BF)
    z_forward(3, 0)
    z_forward(1, 0)
    lhs_ref[0:LOCAL, :] = (
        dotb(ortho, w_hi, ((1,), (0,))) + dotb(ortho, w_lo, ((1,), (0,)))
    ).astype(BF)
    z_forward(2, 0)
    z_last(0, 0)
    for wait in norm_in:
        wait()
    nr2[0] = tree([nr1[e] for e in range(16)])
    norm_in = [
        send(nr2.at[0], nr2.at[f + 1], member(dy, dc), nr2.at[f + 1])
        for f, (dy, dc) in enumerate(group)
    ]
    z_forward(3, 1)
    z_forward(1, 1)
    z_forward(2, 1)
    z_last(0, 1)
    for wait in norm_in:
        wait()
    total = tree([nr2[f] for f in range(8)])
    total = jnp.concatenate([total[i : i + 1] for i in range(4)], axis=1)
    scale = lax.rsqrt(total + 1e-06)
    sub16 = lax.broadcasted_iota(jnp.int32, (16, RANK), 0)
    lane16 = lax.broadcasted_iota(jnp.int32, (16, RANK), 1)
    pick = jnp.where(lane16 == sub16 + r * 16, scale, 0.0)
    o_hi, o_lo = split(jnp.concatenate([ortho.astype(F32) * scale, pick], axis=0))
    lhs_ref[LOCAL : 2 * LOCAL + 16, :] = (
        dotb(o_hi, w_hi, ((1,), (0,)))
        + (dotb(o_hi, w_lo, ((1,), (0,))) + dotb(o_lo, w_hi, ((1,), (0,))))
    ).astype(BF)
    for s in range(2):
        for d in (3, 1, 2):
            z_last(d, s)
    for _, wait in zs.values():
        wait()
    for wait in sent:
        wait()


def gather_call(momentum, gradient, basis):
    anyspace = pl.BlockSpec(memory_space=pl.ANY)
    vmem = pl.BlockSpec(memory_space=pltpu.VMEM)
    scratch = [
        ((2, LOCAL, PART), BF),
        ((2, LOCAL, PART), BF),
        ((LOCAL, HALF), BF),
        ((HALF, 2 * LOCAL), BF),
        ((RANK, HALF), BF),
        ((2, LOCAL, 256), F32),
        ((2, LOCAL, 256), F32),
        ((2, LOCAL, 256), BF),
        ((2, LOCAL, 256), BF),
        ((2, LOCAL, 256), BF),
        ((2, 3, 96, 256), BF),
        ((2, 2 * LOCAL, 256), BF),
        ((10, B, B), F32),
        ((15, 5, 8, B), F32),
        ((10, B, B), F32),
        ((RANK, RANK), F32),
        ((B, B), F32),
        ((2, 4, 2, SEG // 2, 256), BF),
        ((2, 2, SEG // 2, 256), F32),
        ((2, 2, SEG // 2, 256), F32),
        ((2, 2, SEG // 2, 256), BF),
        ((2, 2, 2, SEG // 2, 256), BF),
        ((2, 3, SUB, 256), BF),
        ((16, 8, B), F32),
        ((8, 8, B), F32),
    ]
    return pl.pallas_call(
        gather_kernel,
        out_shape=(
            pltpu.VMEM((LOCAL, COLS), BF),
            pltpu.VMEM((COLS, RANK), BF),
            pltpu.VMEM((2 * LOCAL + 16, RANK), BF),
        ),
        in_specs=[anyspace] * 3,
        out_specs=(vmem,) * 3,
        scratch_shapes=[pltpu.VMEM(s, t) for s, t in scratch]
        + [
            pltpu.SemaphoreType.DMA((10,)),
            pltpu.SemaphoreType.DMA((N_SEMS,)),
            pltpu.SemaphoreType.DMA((N_SEMS,)),
        ],
        compiler_params=pltpu.CompilerParams(
            collective_id=0, has_side_effects=True, vmem_limit_bytes=44 << 20
        ),
        name="project",
    )(momentum, gradient, basis)


def apply_kernel(buf_ref, zt_ref, lhs_ref, mom_ref, bas_ref, upd_ref):
    wide = mom_ref.shape[1]
    cols = rows_at(pl.program_id(0) * wide, wide, 128)
    prod = dotb(lhs_ref[...], zt_ref[cols, :], ((1,), (1,)))
    mom_ref[...] = (buf_ref[:, cols].astype(F32) - 0.2 * prod[:LOCAL]).astype(BF)
    factor = math.sqrt(ROWS * WIDTH / RANK)
    upd_ref[...] = (factor * prod[LOCAL : 2 * LOCAL]).astype(BF)
    bas_ref[...] = prod[2 * LOCAL :].astype(BF)


def apply_call(buf, zt, lhs):
    wide = 1664
    block = pl.BlockSpec((LOCAL, wide), lambda i: (0, i))
    held = [pltpu.with_memory_space_constraint(v, pltpu.VMEM) for v in (buf, zt, lhs)]
    return pl.pallas_call(
        apply_kernel,
        grid=(COLS // wide,),
        out_shape=(
            jax.ShapeDtypeStruct((LOCAL, COLS), BF),
            jax.ShapeDtypeStruct((16, COLS), BF),
            jax.ShapeDtypeStruct((LOCAL, COLS), BF),
        ),
        in_specs=[pl.BlockSpec(memory_space=pltpu.VMEM)] * 3,
        out_specs=(block, pl.BlockSpec((16, wide), lambda i: (0, i)), block),
        compiler_params=pltpu.CompilerParams(vmem_limit_bytes=24 << 20),
        name="apply",
    )(*held)


def local(momentum, gradient, basis):
    return apply_call(*gather_call(momentum, gradient, basis))


def solution(mesh):
    return jax.shard_map(
        local,
        mesh=mesh,
        in_specs=(P("rows", "cols"), P("rows", "cols"), P("rows", "cols")),
        out_specs=(P("rows", "cols"), P("rows", "cols"), P("rows", "cols")),
        check_vma=False,
    )
```

time: 145 us -> 111 us (0.77)
  Pallas kernels: 140 us -> 110 us
  local copies, waits for them, and re-layouts: 3.59 us -> 0 us
    pallas_call x1, Pallas kernels: 127 us -> 102 us  [gather_call(): pl.pallas_call(gather_kernel, out_shape=(pltpu.VMEM((LOCAL, COLS), BF), p...]
    pallas_call x1, Pallas kernels: 13.8 us -> 8.14 us  [apply_call(): pl.pallas_call(apply_kernel, grid=(COLS // wide,), out_shape=(jax.ShapeDt...]
    unnamed x6 -> x0, local copies, waits for them, and re-layouts: 3.59 us -> none
where the time goes in v2:
time: 111 us
  Pallas kernels  110 us (99%)
    pallas_call x1, Pallas kernels, gather_call(): pl.pallas_call(gather_kernel, out_shape=(pltpu.VMEM((LOCAL, COLS), BF), p...  102 us
    pallas_call x1, Pallas kernels, apply_call(): pl.pallas_call(apply_kernel, grid=(COLS // wide,), out_shape=(jax.ShapeDt...  8.14 us

profile of v2, /device:TPU:1, one launch (start us, length us, event | category | flops | bytes accessed | tf_op | source)
XLA Modules:
  0.0 111.1 jit_solution(752461824827885303)
XLA Ops:
  0.6 102.3 %project.1 = (bf16[384,6656]{1,0:T(8,128)(2,1)S(1)}, bf16[6656,512]{1,0:T(8,128)(2,1)S(1)}, bf16[784,512]{1,0:T(8,128)(2,1)S(1)}) custom-call(bf16[384,6656]{1,0:T(8,128)(2,1)} %m_hbm.1, bf16[384,6656]{1,0:T(8,128)(2,1)} %g_hbm.1, bf16[16,6656]{1,0:T(8,128)(2,1)} %basis_hbm.1), custom_call_target="tpu_custom_call" | custom-call | tf_op jit(solution)/shard_map/project/pallas_call | solution.py:701
  103.0 8.1 %apply.1 = (bf16[384,6656]{1,0:T(8,128)(2,1)}, bf16[16,6656]{1,0:T(8,128)(2,1)}, bf16[384,6656]{1,0:T(8,128)(2,1)}) custom-call(bf16[384,6656]{1,0:T(8,128)(2,1)S(1)} %get-tuple-element.6.buf_ref, bf16[6656,512]{1,0:T(8,128)(2,1)S(1)} %get-tuple-element.7.zt_ref, bf16[784,512]{1,0:T(8,128)(2,1)S(1)} %get-tuple-element.8.lhs_ref), custom_call_target="tpu_custom_call" | custom-call | tf_op jit(solution)/shard_map/apply/pallas_call | solution.py:737

commit v3 on v2

--- a/solution.py
+++ b/solution.py
@@ -127,8 +127,8 @@
 
 def gather_kernel(
     m_hbm, g_hbm, basis_hbm, buf_ref, zt_ref, lhs_ref,
-    mbuf, gbuf, side, buf2t, bas, psum, pleft, psend, precv, chip_left, yr, left2,
-    gs, gr, gram, tmat, wmat, zp, zown, zl, zrh, zrf, zr2, nr1, nr2,
+    mbuf, gbuf, side, buf2t, bas, pleft, psend, precv, chip_left, yr, left2,
+    gs, gr, gram, tmat, wmat, zp, zown, zl, zrh, zrf, zr2, nr1, nr2, onehot, ltrue, feed,
     load_sem, send_sem, recv_sem,
 ):
     r = lax.axis_index("rows")
@@ -202,16 +202,19 @@
     for n in range(2):
         for copy in loads[n]:
             copy.start()
-    own_rows = rows_at(r * 16, 16)
     parts = [pl.ds(0, PART), pl.ds(PART, PART)]
-    own_basis = [
-        pltpu.make_async_copy(
-            basis_hbm.at[:, columns(c, n)], bas.at[own_rows, parts[n]], load_sem.at[8 + n]
-        )
-        for n in range(2)
-    ]
-    for copy in own_basis:
-        copy.start()
+
+    def half_of(core):
+        return pl.ds(pl.multiple_of(core * HALF, 128), HALF)
+
+    def chip_rows(a, b):
+        return rows_at(chip(a, b) * 16, 16)
+
+    here = chip_rows(p1, p2)
+    own_basis = pltpu.make_async_copy(
+        basis_hbm.at[:, half_of(c)], bas.at[c, here], load_sem.at[8]
+    )
+    own_basis.start()
 
     barrier = pltpu.get_barrier_semaphore()
     others = [sib, a1p, a1m, a2p, a2m] + [(r, mod4(y + d)) for d in (1, 2, 3)]
@@ -219,22 +222,13 @@
         pl.semaphore_signal(barrier, inc=1, device_id=to, device_id_type=MESH)
     pl.semaphore_wait(barrier, len(others))
 
-    sib_ranks = rows_at((r + 1 - 2 * c) * 16, 16)
-    got = [
-        send(
-            basis_hbm.at[:, columns(1 - c, n)],
-            bas.at[own_rows, parts[n]],
-            sib,
-            bas.at[sib_ranks, parts[n]],
-        )
-        for n in range(2)
-    ]
+    got = send(basis_hbm.at[:, half_of(1 - c)], bas.at[c, here], sib, bas.at[1 - c, here])
 
     def piece(a, b, n):
-        return bas.at[rows_at(chip(a, b) * 32, 32), parts[n]]
+        return bas.at[n, chip_rows(a, b)]
 
     def half_piece(a, b, n, h):
-        return bas.at[rows_at(chip(a, b) * 32 + 16 * h, 16), parts[n]]
+        return bas.at[n, chip_rows(a, b), parts[h]]
 
     def at1(d):
         return mod4(p1 + d)
@@ -242,26 +236,48 @@
     def at2(d):
         return mod4(p2 + d)
 
-    first = []
-    for n in range(2):
-        own_basis[n].wait()
-        got[n]()
-        mine = piece(p1, p2, n)
-        first.append(
+    own_basis.wait()
+    got()
+    first = [None, None]
+    second = [[], []]
+    opposite1 = [None, None]
+
+    def both2(d, n):
+        a = at1(d)
+        ref = piece(a, p2, n)
+        second[n].append(
             (
-                send(mine, mine, a1p, piece(at1(-1), p2, n)),
-                send(mine, mine, a1m, piece(at1(1), p2, n)),
+                send(ref, ref, a2p, piece(a, at2(-1), n)),
+                send(ref, ref, a2m, piece(a, at2(1), n)),
             )
         )
 
-    def both2(a, n):
-        ref = piece(a, p2, n)
-        return (
-            send(ref, ref, a2p, piece(a, at2(-1), n)),
-            send(ref, ref, a2m, piece(a, at2(1), n)),
+    def start(n):
+        mine = piece(p1, p2, n)
+        first[n] = (
+            send(mine, mine, a1p, piece(at1(-1), p2, n)),
+            send(mine, mine, a1m, piece(at1(1), p2, n)),
         )
-
-    second = [[both2(p1, n)] for n in range(2)]
+        both2(0, n)
+
+    def pass_on(n):
+        from_m, from_p = first[n]
+        from_m()
+        ref = half_piece(at1(-1), p2, n, 0)
+        opp0 = send(ref, ref, a1p, half_piece(at1(2), p2, n, 0))
+        both2(-1, n)
+        from_p()
+        ref = half_piece(at1(1), p2, n, 1)
+        opp1 = send(ref, ref, a1m, half_piece(at1(2), p2, n, 1))
+        both2(1, n)
+        opposite1[n] = (opp0, opp1)
+
+    def opposite(n):
+        for wait in opposite1[n]:
+            wait()
+        both2(2, n)
+
+    start(0)
 
     def add_loaded(n):
         for copy in loads[n]:
@@ -298,27 +314,6 @@
 
         lax.fori_loop(0, PART // 128, step, 0)
 
-    add_loaded(0)
-    swapped = [send_buffer(0)]
-    opposite1 = []
-    for n in range(2):
-        from_m, from_p = first[n]
-        from_m()
-        ref = half_piece(at1(-1), p2, n, 0)
-        opp0 = send(ref, ref, a1p, half_piece(at1(2), p2, n, 0))
-        second[n].append(both2(at1(-1), n))
-        from_p()
-        ref = half_piece(at1(1), p2, n, 1)
-        opp1 = send(ref, ref, a1m, half_piece(at1(2), p2, n, 1))
-        second[n].append(both2(at1(1), n))
-        opposite1.append((opp0, opp1))
-    add_loaded(1)
-    swapped.append(send_buffer(1))
-    for n in range(2):
-        for wait in opposite1[n]:
-            wait()
-        second[n].append(both2(at1(2), n))
-    add_loaded(2)
     last = [[], []]
     offsets = (0, -1, 1, 2)
 
@@ -332,172 +327,7 @@
         ref = half_piece(a, at2(1), n, 1)
         last[n].append(send(ref, ref, a2m, half_piece(a, at2(2), n, 1)))
 
-    forward2(0, 0)
-    forward2(0, 1)
-    add_loaded(3)
-    forward2(0, 2)
-    forward2(0, 3)
-    forward2(1, 0)
-    turn(0, True)
-    forward2(1, 1)
-    turn(1, True)
-    swapped[0]()
-    turn(0, False)
-    forward2(1, 2)
-    swapped[1]()
-    turn(1, False)
-    forward2(1, 3)
-
     ranks = [pl.ds(0, 256), pl.ds(256, 256)]
-
-    def left_part(mine, n, s):
-        rows = buf_ref[:, columns(c, n)] if mine else side[:, parts[n]]
-        return dotb(rows, bas[ranks[s], parts[n]], ((1,), (1,)))
-
-    for wait in last[0]:
-        wait()
-    for s in range(2):
-        psum[s] = left_part(False, 0, s)
-        pleft[s] = left_part(True, 0, s)
-    for wait in last[1]:
-        wait()
-    paired = []
-    for s in range(2):
-        psend[s] = (psum[s] + left_part(False, 1, s)).astype(BF)
-        paired.append(send(psend.at[s], precv.at[s], sib, precv.at[s]))
-        pleft[s] = pleft[s] + left_part(True, 1, s)
-
-    def along_y(d):
-        return (r, mod4(y + d))
-
-    def left_rows(core, d):
-        return rows_at(core * LOCAL + mod4(y + d) * 96, 96)
-
-    summed = []
-    for s in range(2):
-        paired[s]()
-        total = pleft[s] + precv[s].astype(F32)
-        pleft[s] = total
-        chip_left[s] = total.astype(BF)
-        summed.append(
-            [
-                send(
-                    chip_left.at[s, rows_at(mod4(y + d) * 96, 96)],
-                    yr.at[s, d - 1],
-                    along_y(d),
-                    yr.at[s, d - 1],
-                )
-                for d in (2, 1, 3)
-            ]
-        )
-    spread, pairs = [], []
-    for s in range(2):
-        for wait in summed[s]:
-            wait()
-        total = pleft[s, rows_at(y * 96, 96), :]
-        for d in range(3):
-            total = total + yr[s, d].astype(F32)
-        left2[s, left_rows(c, 0), :] = total.astype(BF)
-        ref = left2.at[s, left_rows(c, 0)]
-        spread.append(
-            {d: send(ref, ref, along_y(d), left2.at[s, left_rows(c, -d)]) for d in (2, 1, 3)}
-        )
-        pairs.append([send(ref, ref, sib, left2.at[s, left_rows(1 - c, 0)])])
-
-    def left_done(s):
-        for d in (1, 3, 2):
-            spread[s][d]()
-            ref = left2.at[s, left_rows(c, -d)]
-            pairs[s].append(send(ref, ref, sib, left2.at[s, left_rows(1 - c, -d)]))
-        for wait in pairs[s]:
-            wait()
-
-    def z_value(d, h, s):
-        at = rows_at(mod4(p1 + d) * SEG + (SEG // 2) * h, SEG // 2)
-        return dotb(buf2t[at, :], left2[s], ((1,), (0,)))
-
-    ways = (a1p, a1m)
-    z_half = [[], []]
-    z_full = [[], []]
-
-    def z_first(s):
-        for w in range(2):
-            zp[s, 2, w] = z_value(2, w, s).astype(BF)
-            z_half[s].append(send(zp.at[s, 2, w], zrh.at[s, w], ways[w], zrh.at[s, w]))
-
-    def z_middle(s):
-        for w, (d, h) in enumerate(((1, 1), (3, 0))):
-            zp[s, d, h] = z_value(d, h, s).astype(BF)
-            z_full[s].append(send(zp.at[s, d, h], zrf.at[s, w, h], ways[w], zrf.at[s, w, h]))
-
-    def z_prepare(s):
-        for w, (d, h) in enumerate(((1, 0), (3, 1))):
-            zl[s, w] = z_value(d, h, s)
-
-    def z_add(s):
-        for w, (d, h) in enumerate(((1, 0), (3, 1))):
-            z_half[s][w]()
-            zp[s, d, h] = (zl[s, w] + zrh[s, w].astype(F32)).astype(BF)
-            z_full[s].append(send(zp.at[s, d, h], zrf.at[s, w, h], ways[w], zrf.at[s, w, h]))
-
-    def z_own(s):
-        for h in range(2):
-            zown[s, h] = z_value(0, h, s)
-
-    left_done(0)
-    z_first(0)
-    left_done(1)
-
-    blocks = [(i, j) for i in range(4) for j in range(i, 4)]
-
-    def left_block(i):
-        return left2[i // 2, :, 128 * (i % 2) : 128 * (i % 2) + 128]
-
-    for b, (i, j) in enumerate(blocks):
-        gs[b] = dotb(left_block(i), left_block(j), ((0,), (0,)))
-
-    def tile(j):
-        return pl.ds(lax.rem(j, 2) * 5, 5), rows_at(c * 64 + lax.div(j, 2) * 8, 8, 8)
-
-    gram_in = []
-    for e, (dx, dz) in enumerate(plane):
-        to = tile(mod4(x + dx) * 4 + mod4(z + dz))
-        gram_in.append(send(gs.at[to], gr.at[e], peer(dx, dz), gr.at[e]))
-    z_first(1)
-    z_middle(0)
-    for wait in gram_in:
-        wait()
-    mine = tile(x * 4 + z)
-    gram[mine] = gs[mine] + tree([gr[e] for e in range(15)] + [jnp.zeros((5, 8, B), F32)])
-    gathered = []
-    for dx, dz in plane:
-        ref = gram.at[mine]
-        gathered.append(send(ref, ref, peer(dx, dz), gram.at[tile(source_chip(dx, dz))]))
-    z_middle(1)
-    z_prepare(0)
-    z_add(0)
-    z_prepare(1)
-    z_add(1)
-    z_own(0)
-    z_own(1)
-    for wait in gathered:
-        wait()
-    ref = gram.at[:, rows_at(c * 64, 64)]
-    send(ref, ref, sib, gram.at[:, rows_at((1 - c) * 64, 64)])()
-
-    on = lax.broadcasted_iota(jnp.int32, (B, B), 0) == lax.broadcasted_iota(jnp.int32, (B, B), 1)
-    across, down = [], []
-    for i in range(4):
-        diag = jnp.where(on, gram[blocks.index((i, i))], 0.0)
-        across.append(lax.rsqrt(jnp.sum(diag, axis=0, keepdims=True)))
-        down.append(lax.rsqrt(jnp.sum(diag, axis=1, keepdims=True)))
-    for i in range(4):
-        for j in range(4):
-            if j < i:
-                block = jnp.zeros((B, B), F32)
-            else:
-                block = gram[blocks.index((i, j))] * down[i] * across[j]
-            tmat[B * i : B * i + B, B * j : B * j + B] = block
 
     def sub_rows(a, b):
         return rows_at(c * HALF + a * SEG + b * SUB, SUB)
@@ -591,17 +421,212 @@
             wait()
         zs[s, 2, d][0]()
 
+    for n in range(2):
+        k = lax.broadcasted_iota(jnp.int32, (256, RANK), 0)
+        rank = lax.shift_right_logical(k, 4) * 32 + (k & 15) + 16 * n
+        hit = lax.broadcasted_iota(jnp.int32, (256, RANK), 1) == rank
+        onehot[n] = jnp.where(hit, 1.0, 0.0).astype(BF)
+
+    paired, summed, spread, pairs = [], [], [], []
+
+    def left_pair(s):
+        for wait in last[s]:
+            wait()
+        psend[s] = dotb(side[...], bas[s], ((1,), (1,))).astype(BF)
+        paired.append(send(psend.at[s], precv.at[s], sib, precv.at[s]))
+        pleft[s] = dotb(buf_ref[:, half_of(c)], bas[s], ((1,), (1,)))
+
+    def along_y(d):
+        return (r, mod4(y + d))
+
+    def left_rows(core, d):
+        return rows_at(core * LOCAL + mod4(y + d) * 96, 96)
+
+    def left_sum(s):
+        paired[s]()
+        total = pleft[s] + precv[s].astype(F32)
+        pleft[s] = total
+        chip_left[s] = total.astype(BF)
+        summed.append(
+            [
+                send(
+                    chip_left.at[s, rows_at(mod4(y + d) * 96, 96)],
+                    yr.at[s, d - 1],
+                    along_y(d),
+                    yr.at[s, d - 1],
+                )
+                for d in (2, 1, 3)
+            ]
+        )
+
+    def left_spread(s):
+        for wait in summed[s]:
+            wait()
+        total = pleft[s, rows_at(y * 96, 96), :]
+        for d in range(3):
+            total = total + yr[s, d].astype(F32)
+        left2[s, left_rows(c, 0), :] = total.astype(BF)
+        ref = left2.at[s, left_rows(c, 0)]
+        spread.append(
+            {d: send(ref, ref, along_y(d), left2.at[s, left_rows(c, -d)]) for d in (2, 1, 3)}
+        )
+        pairs.append([send(ref, ref, sib, left2.at[s, left_rows(1 - c, 0)])])
+
+    def left_done(s):
+        for d in (1, 3, 2):
+            spread[s][d]()
+            ref = left2.at[s, left_rows(c, -d)]
+            pairs[s].append(send(ref, ref, sib, left2.at[s, left_rows(1 - c, -d)]))
+        for wait in pairs[s]:
+            wait()
+
+    def z_value(d, h, s):
+        at = rows_at(mod4(p1 + d) * SEG + (SEG // 2) * h, SEG // 2)
+        return dotb(buf2t[at, :], left2[s], ((1,), (0,)))
+
+    ways = (a1p, a1m)
+    z_half = [[], []]
+    z_full = [[], []]
+
+    def z_first(s):
+        for w in range(2):
+            zp[s, 2, w] = z_value(2, w, s).astype(BF)
+            z_half[s].append(send(zp.at[s, 2, w], zrh.at[s, w], ways[w], zrh.at[s, w]))
+
+    def z_middle(s):
+        for w, (d, h) in enumerate(((1, 1), (3, 0))):
+            zp[s, d, h] = z_value(d, h, s).astype(BF)
+            z_full[s].append(send(zp.at[s, d, h], zrf.at[s, w, h], ways[w], zrf.at[s, w, h]))
+
+    def z_prepare(s):
+        for w, (d, h) in enumerate(((1, 0), (3, 1))):
+            zl[s, w] = z_value(d, h, s)
+
+    def z_add(s):
+        for w, (d, h) in enumerate(((1, 0), (3, 1))):
+            z_half[s][w]()
+            zp[s, d, h] = (zl[s, w] + zrh[s, w].astype(F32)).astype(BF)
+            z_full[s].append(send(zp.at[s, d, h], zrf.at[s, w, h], ways[w], zrf.at[s, w, h]))
+
+    def z_own(s):
+        for h in range(2):
+            zown[s, h] = z_value(0, h, s)
+
+    add_loaded(0)
+    swapped = [send_buffer(0)]
+    swap_sent = [sent.pop()]
+    pass_on(0)
+    start(1)
+    add_loaded(1)
+    swapped.append(send_buffer(1))
+    swap_sent.append(sent.pop())
+    opposite(0)
+    add_loaded(2)
+    forward2(0, 0)
+    forward2(0, 1)
+    forward2(0, 2)
+    pass_on(1)
+    add_loaded(3)
+    forward2(0, 3)
+    opposite(1)
+    turn(0, True)
+    turn(1, True)
+    forward2(1, 0)
+    for wait in swapped:
+        wait()
+    left_pair(0)
+    forward2(1, 1)
+    left_sum(0)
+    forward2(1, 2)
+    turn(0, False)
+    turn(1, False)
+    forward2(1, 3)
+    left_spread(0)
+    left_pair(1)
+    left_sum(1)
+    left_done(0)
+    z_first(0)
+    z_middle(0)
+    z_prepare(0)
+    left_spread(1)
+    z_add(0)
+    z_own(0)
+    left_done(1)
+
+    blocks = [(i, j) for i in range(4) for j in range(i, 4)]
+
+    ltrue[...] = (
+        dotb(left2[0], onehot[0], ((1,), (0,))) + dotb(left2[1], onehot[1], ((1,), (0,)))
+    ).astype(BF)
+
+    def left_block(i):
+        return ltrue[:, B * i : B * i + B]
+
+    for b, (i, j) in enumerate(blocks):
+        gs[b] = dotb(left_block(i), left_block(j), ((0,), (0,)))
+
+    def tile(j):
+        return pl.ds(lax.rem(j, 2) * 5, 5), rows_at(c * 64 + lax.div(j, 2) * 8, 8, 8)
+
+    gram_in = []
+    for e, (dx, dz) in enumerate(plane):
+        to = tile(mod4(x + dx) * 4 + mod4(z + dz))
+        gram_in.append(send(gs.at[to], gr.at[e], peer(dx, dz), gr.at[e]))
+    z_sum1(0)
+    z_first(1)
+    for wait in gram_in:
+        wait()
+    mine = tile(x * 4 + z)
+    gram[mine] = gs[mine] + tree([gr[e] for e in range(15)] + [jnp.zeros((5, 8, B), F32)])
+    gathered = []
+    for dx, dz in plane:
+        ref = gram.at[mine]
+        gathered.append(send(ref, ref, peer(dx, dz), gram.at[tile(source_chip(dx, dz))]))
+    z_middle(1)
+    z_sum2(0)
+    z_prepare(1)
+    z_add(1)
+    z_own(1)
+    for wait in gathered:
+        wait()
+    ref = gram.at[:, rows_at(c * 64, 64)]
+    pair_gram = send(ref, ref, sib, gram.at[:, rows_at((1 - c) * 64, 64)])
+    z_forward(0, 0)
+    pair_gram()
+
+    on = lax.broadcasted_iota(jnp.int32, (B, B), 0) == lax.broadcasted_iota(jnp.int32, (B, B), 1)
+    across, down = [], []
+    for i in range(4):
+        diag = jnp.where(on, gram[blocks.index((i, i))], 0.0)
+        across.append(lax.rsqrt(jnp.sum(diag, axis=0, keepdims=True)))
+        down.append(lax.rsqrt(jnp.sum(diag, axis=1, keepdims=True)))
+    for i in range(4):
+        for j in range(4):
+            if j < i:
+                block = jnp.zeros((B, B), F32)
+            else:
+                block = gram[blocks.index((i, j))] * down[i] * across[j]
+            tmat[B * i : B * i + B, B * j : B * j + B] = block
+
     steps = {
-        (0, 5): lambda: z_sum1(0),
-        (1, 1): lambda: z_sum1(1),
-        (2, 0): lambda: z_sum2(0),
-        (2, 6): lambda: z_sum2(1),
-        (3, 0): lambda: z_forward(0, 0),
-        (3, 2): lambda: z_gather2(1, 0),
-        (3, 3): lambda: z_gather2(3, 0),
-        (3, 4): lambda: z_gather2(2, 0),
-        (3, 5): lambda: z_forward(0, 1),
-        (3, 7): lambda: z_gather2(1, 1),
+        (0, 0): lambda: z_sum1(1),
+        (0, 1): lambda: z_gather2(1, 0),
+        (0, 2): lambda: z_gather2(3, 0),
+        (0, 3): lambda: z_gather2(2, 0),
+        (0, 7): lambda: z_last(0, 0),
+        (1, 2): lambda: z_sum2(1),
+        (1, 4): lambda: z_forward(3, 0),
+        (1, 5): lambda: z_forward(1, 0),
+        (1, 6): lambda: z_forward(2, 0),
+        (2, 1): lambda: z_forward(0, 1),
+        (2, 4): lambda: z_gather2(1, 1),
+        (2, 5): lambda: z_gather2(3, 1),
+        (2, 6): lambda: z_gather2(2, 1),
+        (2, 7): lambda: z_last(3, 0),
+        (3, 0): lambda: z_last(1, 0),
+        (3, 1): lambda: z_last(2, 0),
+        (3, 2): lambda: z_last(0, 1),
+        (3, 7): lambda: z_forward(3, 1),
     }
 
     def hook(k, part):
@@ -613,7 +638,12 @@
     ri = lax.broadcasted_iota(jnp.int32, (RANK, RANK), 0)
     ci = lax.broadcasted_iota(jnp.int32, (RANK, RANK), 1)
     tmat[...] = jnp.where(ci <= ri, tmat[...], 0.0) * jnp.concatenate(across, axis=1)
-    w_hi, w_lo = split(tmat[...])
+    w_hi, w_lo = [
+        jnp.concatenate(
+            [dotb(w, onehot[n], ((1,), (1,))).astype(BF) for n in range(2)], axis=1
+        )
+        for w in split(tmat[...])
+    ]
 
     shard = zt_ref[sub_rows(p1, p2), :]
     right = dotb(shard, w_hi, ((1,), (1,))) + dotb(shard, w_lo, ((1,), (1,)))
@@ -624,17 +654,11 @@
         send(nr1.at[0], nr1.at[e + 1], peer(dx, dz), nr1.at[e + 1])
         for e, (dx, dz) in enumerate(plane)
     ]
-    z_gather2(3, 1)
-    z_gather2(2, 1)
+    z_forward(1, 1)
     own_left = jnp.concatenate([left2[0, my_rows, :], left2[1, my_rows, :]], axis=1)
     ortho = (dotb(own_left, w_hi, ((1,), (1,))) + dotb(own_left, w_lo, ((1,), (1,)))).astype(BF)
-    z_forward(3, 0)
-    z_forward(1, 0)
-    lhs_ref[0:LOCAL, :] = (
-        dotb(ortho, w_hi, ((1,), (0,))) + dotb(ortho, w_lo, ((1,), (0,)))
-    ).astype(BF)
-    z_forward(2, 0)
-    z_last(0, 0)
+    z_forward(2, 1)
+    feed[...] = (dotb(ortho, w_hi, ((1,), (0,))) + dotb(ortho, w_lo, ((1,), (0,)))).astype(BF)
     for wait in norm_in:
         wait()
     nr2[0] = tree([nr1[e] for e in range(16)])
@@ -642,10 +666,17 @@
         send(nr2.at[0], nr2.at[f + 1], member(dy, dc), nr2.at[f + 1])
         for f, (dy, dc) in enumerate(group)
     ]
-    z_forward(3, 1)
-    z_forward(1, 1)
-    z_forward(2, 1)
-    z_last(0, 1)
+    for d in (3, 1, 2):
+        z_last(d, 1)
+    for _, wait in zs.values():
+        wait()
+
+    for wait in swap_sent:
+        wait()
+    for n in range(COLS // 512):
+        at = pl.ds(512 * n, 512)
+        prod = dotb(feed[...], zt_ref[at, :], ((1,), (1,)))
+        buf_ref[:, at] = (buf_ref[:, at].astype(F32) - 0.2 * prod).astype(BF)
     for wait in norm_in:
         wait()
     total = tree([nr2[f] for f in range(8)])
@@ -655,15 +686,10 @@
     lane16 = lax.broadcasted_iota(jnp.int32, (16, RANK), 1)
     pick = jnp.where(lane16 == sub16 + r * 16, scale, 0.0)
     o_hi, o_lo = split(jnp.concatenate([ortho.astype(F32) * scale, pick], axis=0))
-    lhs_ref[LOCAL : 2 * LOCAL + 16, :] = (
+    lhs_ref[...] = (
         dotb(o_hi, w_hi, ((1,), (0,)))
         + (dotb(o_hi, w_lo, ((1,), (0,))) + dotb(o_lo, w_hi, ((1,), (0,))))
     ).astype(BF)
-    for s in range(2):
-        for d in (3, 1, 2):
-            z_last(d, s)
-    for _, wait in zs.values():
-        wait()
     for wait in sent:
         wait()
 
@@ -676,8 +702,7 @@
         ((2, LOCAL, PART), BF),
         ((LOCAL, HALF), BF),
         ((HALF, 2 * LOCAL), BF),
-        ((RANK, HALF), BF),
-        ((2, LOCAL, 256), F32),
+        ((2, 256, HALF), BF),
         ((2, LOCAL, 256), F32),
         ((2, LOCAL, 256), BF),
         ((2, LOCAL, 256), BF),
@@ -697,19 +722,22 @@
         ((2, 3, SUB, 256), BF),
         ((16, 8, B), F32),
         ((8, 8, B), F32),
+        ((2, 256, RANK), BF),
+        ((2 * LOCAL, RANK), BF),
+        ((LOCAL, RANK), BF),
     ]
     return pl.pallas_call(
         gather_kernel,
         out_shape=(
             pltpu.VMEM((LOCAL, COLS), BF),
             pltpu.VMEM((COLS, RANK), BF),
-            pltpu.VMEM((2 * LOCAL + 16, RANK), BF),
+            pltpu.VMEM((LOCAL + 16, RANK), BF),
         ),
         in_specs=[anyspace] * 3,
         out_specs=(vmem,) * 3,
         scratch_shapes=[pltpu.VMEM(s, t) for s, t in scratch]
         + [
-            pltpu.SemaphoreType.DMA((10,)),
+            pltpu.SemaphoreType.DMA((9,)),
             pltpu.SemaphoreType.DMA((N_SEMS,)),
             pltpu.SemaphoreType.DMA((N_SEMS,)),
         ],
@@ -720,30 +748,41 @@
     )(momentum, gradient, basis)
 
 
-def apply_kernel(buf_ref, zt_ref, lhs_ref, mom_ref, bas_ref, upd_ref):
-    wide = mom_ref.shape[1]
-    cols = rows_at(pl.program_id(0) * wide, wide, 128)
-    prod = dotb(lhs_ref[...], zt_ref[cols, :], ((1,), (1,)))
-    mom_ref[...] = (buf_ref[:, cols].astype(F32) - 0.2 * prod[:LOCAL]).astype(BF)
+def apply_kernel(mom_ref, zt_ref, lhs_ref, mom_hbm, bas_hbm, upd_hbm, bas, upd, sem):
+    first = pltpu.make_async_copy(mom_ref, mom_hbm, sem.at[0])
+    first.start()
     factor = math.sqrt(ROWS * WIDTH / RANK)
-    upd_ref[...] = (factor * prod[LOCAL : 2 * LOCAL]).astype(BF)
-    bas_ref[...] = prod[2 * LOCAL :].astype(BF)
-
-
-def apply_call(buf, zt, lhs):
-    wide = 1664
-    block = pl.BlockSpec((LOCAL, wide), lambda i: (0, i))
-    held = [pltpu.with_memory_space_constraint(v, pltpu.VMEM) for v in (buf, zt, lhs)]
+    copies = []
+    for n in range(COLS // 512):
+        at = pl.ds(512 * n, 512)
+        prod = dotb(lhs_ref[...], zt_ref[at, :], ((1,), (1,)))
+        upd[:, at] = (factor * prod[:LOCAL]).astype(BF)
+        bas[:, at] = prod[LOCAL:].astype(BF)
+        copies.append(pltpu.make_async_copy(upd.at[:, at], upd_hbm.at[:, at], sem.at[n + 2]))
+        copies[-1].start()
+    copies.append(pltpu.make_async_copy(bas, bas_hbm, sem.at[1]))
+    copies[-1].start()
+    first.wait()
+    for copy in copies:
+        copy.wait()
+
+
+def apply_call(mom, zt, lhs):
+    held = [pltpu.with_memory_space_constraint(v, pltpu.VMEM) for v in (mom, zt, lhs)]
     return pl.pallas_call(
         apply_kernel,
-        grid=(COLS // wide,),
         out_shape=(
             jax.ShapeDtypeStruct((LOCAL, COLS), BF),
             jax.ShapeDtypeStruct((16, COLS), BF),
             jax.ShapeDtypeStruct((LOCAL, COLS), BF),
         ),
         in_specs=[pl.BlockSpec(memory_space=pltpu.VMEM)] * 3,
-        out_specs=(block, pl.BlockSpec((16, wide), lambda i: (0, i)), block),
+        out_specs=[pl.BlockSpec(memory_space=pl.ANY)] * 3,
+        scratch_shapes=[
+            pltpu.VMEM((16, COLS), BF),
+            pltpu.VMEM((LOCAL, COLS), BF),
+            pltpu.SemaphoreType.DMA((2 + COLS // 512,)),
+        ],
         compiler_params=pltpu.CompilerParams(vmem_limit_bytes=24 << 20),
         name="apply",
     )(*held)

time: 111 us -> 112 us (level)
    pallas_call x1, Pallas kernels: 102 us -> 107 us  [gather_call(): pl.pallas_call(gather_kernel, out_shape=(pltpu.VMEM((LOCAL, COLS), BF), p...]
    pallas_call x1, Pallas kernels: 8.14 us -> 4.03 us  [apply_call(): pl.pallas_call(apply_kernel, out_shape=(jax.ShapeDtypeStruct((LOCAL, COLS...]
where the time goes in v3:
time: 112 us
  Pallas kernels  111 us (99%)
    pallas_call x1, Pallas kernels, gather_call(): pl.pallas_call(gather_kernel, out_shape=(pltpu.VMEM((LOCAL, COLS), BF), p...  107 us
    pallas_call x1, Pallas kernels, apply_call(): pl.pallas_call(apply_kernel, out_shape=(jax.ShapeDtypeStruct((LOCAL, COLS...  4.03 us

profile of v3, /device:TPU:1, one launch (start us, length us, event | category | flops | bytes accessed | tf_op | source)
XLA Modules:
  0.0 112.3 jit_solution(3697646886238812912)
XLA Ops:
  0.6 107.5 %project.1 = (bf16[384,6656]{1,0:T(8,128)(2,1)S(1)}, bf16[6656,512]{1,0:T(8,128)(2,1)S(1)}, bf16[400,512]{1,0:T(8,128)(2,1)S(1)}) custom-call(bf16[384,6656]{1,0:T(8,128)(2,1)} %m_hbm.1, bf16[384,6656]{1,0:T(8,128)(2,1)} %g_hbm.1, bf16[16,6656]{1,0:T(8,128)(2,1)} %basis_hbm.1), custom_call_target="tpu_custom_call" | custom-call | tf_op jit(solution)/shard_map/project/pallas_call | solution.py:729
  108.1 4.0 %apply.1 = (bf16[384,6656]{1,0:T(8,128)(2,1)}, bf16[16,6656]{1,0:T(8,128)(2,1)}, bf16[384,6656]{1,0:T(8,128)(2,1)}) custom-call(bf16[384,6656]{1,0:T(8,128)(2,1)S(1)} %get-tuple-element.6.mom_ref, bf16[6656,512]{1,0:T(8,128)(2,1)S(1)} %get-tuple-element.7.zt_ref, bf16[400,512]{1,0:T(8,128)(2,1)S(1)} %get-tuple-element.8.lhs_ref), custom_call_target="tpu_custom_call" | custom-call | tf_op jit(solution)/shard_map/apply/pallas_call | solution.py:772

commit v4 on v3

--- a/solution.py
+++ b/solution.py
@@ -128,7 +128,7 @@
 def gather_kernel(
     m_hbm, g_hbm, basis_hbm, buf_ref, zt_ref, lhs_ref,
     mbuf, gbuf, side, buf2t, bas, pleft, psend, precv, chip_left, yr, left2,
-    gs, gr, gram, tmat, wmat, zp, zown, zl, zrh, zrf, zr2, nr1, nr2, onehot, ltrue, feed,
+    gs, gr, gram, tmat, wmat, zp, zown, zl, zrh, zrf, zr2, nr1, nr2, onehot, ltrue,
     load_sem, send_sem, recv_sem,
 ):
     r = lax.axis_index("rows")
@@ -217,7 +217,8 @@
     own_basis.start()
 
     barrier = pltpu.get_barrier_semaphore()
-    others = [sib, a1p, a1m, a2p, a2m] + [(r, mod4(y + d)) for d in (1, 2, 3)]
+    a1o = (device(mod4(p1 + 2), p2), y)
+    others = [sib, a1p, a1m, a1o, a2p, a2m] + [(r, mod4(y + d)) for d in (1, 2, 3)]
     for to in others:
         pl.semaphore_signal(barrier, inc=1, device_id=to, device_id_type=MESH)
     pl.semaphore_wait(barrier, len(others))
@@ -240,7 +241,6 @@
     got()
     first = [None, None]
     second = [[], []]
-    opposite1 = [None, None]
 
     def both2(d, n):
         a = at1(d)
@@ -254,30 +254,19 @@
 
     def start(n):
         mine = piece(p1, p2, n)
-        first[n] = (
-            send(mine, mine, a1p, piece(at1(-1), p2, n)),
-            send(mine, mine, a1m, piece(at1(1), p2, n)),
-        )
+        first[n] = {
+            d: send(mine, mine, to, piece(at1(d), p2, n))
+            for d, to in ((-1, a1p), (1, a1m), (2, a1o))
+        }
         both2(0, n)
 
     def pass_on(n):
-        from_m, from_p = first[n]
-        from_m()
-        ref = half_piece(at1(-1), p2, n, 0)
-        opp0 = send(ref, ref, a1p, half_piece(at1(2), p2, n, 0))
-        both2(-1, n)
-        from_p()
-        ref = half_piece(at1(1), p2, n, 1)
-        opp1 = send(ref, ref, a1m, half_piece(at1(2), p2, n, 1))
-        both2(1, n)
-        opposite1[n] = (opp0, opp1)
-
-    def opposite(n):
-        for wait in opposite1[n]:
-            wait()
-        both2(2, n)
+        for d in (-1, 1, 2):
+            first[n][d]()
+            both2(d, n)
 
     start(0)
+    start(1)
 
     def add_loaded(n):
         for copy in loads[n]:
@@ -514,43 +503,35 @@
 
     add_loaded(0)
     swapped = [send_buffer(0)]
-    swap_sent = [sent.pop()]
-    pass_on(0)
-    start(1)
     add_loaded(1)
     swapped.append(send_buffer(1))
-    swap_sent.append(sent.pop())
-    opposite(0)
     add_loaded(2)
+    add_loaded(3)
+    pass_on(0)
+    turn(0, True)
+    pass_on(1)
+    turn(1, True)
     forward2(0, 0)
-    forward2(0, 1)
-    forward2(0, 2)
-    pass_on(1)
-    add_loaded(3)
-    forward2(0, 3)
-    opposite(1)
-    turn(0, True)
-    turn(1, True)
     forward2(1, 0)
     for wait in swapped:
         wait()
+    turn(0, False)
+    forward2(0, 1)
+    turn(1, False)
+    forward2(0, 2)
+    forward2(0, 3)
+    forward2(1, 1)
+    forward2(1, 2)
+    forward2(1, 3)
     left_pair(0)
-    forward2(1, 1)
     left_sum(0)
-    forward2(1, 2)
-    turn(0, False)
-    turn(1, False)
-    forward2(1, 3)
-    left_spread(0)
     left_pair(1)
     left_sum(1)
+    left_spread(0)
+    left_spread(1)
     left_done(0)
     z_first(0)
     z_middle(0)
-    z_prepare(0)
-    left_spread(1)
-    z_add(0)
-    z_own(0)
     left_done(1)
 
     blocks = [(i, j) for i in range(4) for j in range(i, 4)]
@@ -563,41 +544,44 @@
         return ltrue[:, B * i : B * i + B]
 
     for b, (i, j) in enumerate(blocks):
-        gs[b] = dotb(left_block(i), left_block(j), ((0,), (0,)))
+        gs[b] = dotb(left_block(i), left_block(j), ((0,), (0,))).astype(BF)
+    for b in (10, 11):
+        gs[b] = jnp.zeros((B, B), BF)
 
     def tile(j):
-        return pl.ds(lax.rem(j, 2) * 5, 5), rows_at(c * 64 + lax.div(j, 2) * 8, 8, 8)
+        return pl.ds(lax.rem(j, 4) * 3, 3), rows_at(c * 64 + lax.div(j, 4) * 16, 16)
 
     gram_in = []
     for e, (dx, dz) in enumerate(plane):
         to = tile(mod4(x + dx) * 4 + mod4(z + dz))
         gram_in.append(send(gs.at[to], gr.at[e], peer(dx, dz), gr.at[e]))
-    z_sum1(0)
+    z_prepare(0)
+    z_add(0)
     z_first(1)
+    z_middle(1)
     for wait in gram_in:
         wait()
     mine = tile(x * 4 + z)
-    gram[mine] = gs[mine] + tree([gr[e] for e in range(15)] + [jnp.zeros((5, 8, B), F32)])
+    gram[mine] = tree([v.astype(F32) for v in [gs[mine]] + [gr[e] for e in range(15)]]).astype(BF)
     gathered = []
     for dx, dz in plane:
         ref = gram.at[mine]
         gathered.append(send(ref, ref, peer(dx, dz), gram.at[tile(source_chip(dx, dz))]))
-    z_middle(1)
-    z_sum2(0)
     z_prepare(1)
+    z_own(0)
+    z_own(1)
+    z_sum1(0)
     z_add(1)
-    z_own(1)
     for wait in gathered:
         wait()
     ref = gram.at[:, rows_at(c * 64, 64)]
     pair_gram = send(ref, ref, sib, gram.at[:, rows_at((1 - c) * 64, 64)])
-    z_forward(0, 0)
     pair_gram()
 
     on = lax.broadcasted_iota(jnp.int32, (B, B), 0) == lax.broadcasted_iota(jnp.int32, (B, B), 1)
     across, down = [], []
     for i in range(4):
-        diag = jnp.where(on, gram[blocks.index((i, i))], 0.0)
+        diag = jnp.where(on, gram[blocks.index((i, i))].astype(F32), 0.0)
         across.append(lax.rsqrt(jnp.sum(diag, axis=0, keepdims=True)))
         down.append(lax.rsqrt(jnp.sum(diag, axis=1, keepdims=True)))
     for i in range(4):
@@ -605,28 +589,26 @@
             if j < i:
                 block = jnp.zeros((B, B), F32)
             else:
-                block = gram[blocks.index((i, j))] * down[i] * across[j]
+                block = gram[blocks.index((i, j))].astype(F32) * down[i] * across[j]
             tmat[B * i : B * i + B, B * j : B * j + B] = block
 
     steps = {
-        (0, 0): lambda: z_sum1(1),
-        (0, 1): lambda: z_gather2(1, 0),
-        (0, 2): lambda: z_gather2(3, 0),
-        (0, 3): lambda: z_gather2(2, 0),
-        (0, 7): lambda: z_last(0, 0),
-        (1, 2): lambda: z_sum2(1),
-        (1, 4): lambda: z_forward(3, 0),
-        (1, 5): lambda: z_forward(1, 0),
-        (1, 6): lambda: z_forward(2, 0),
-        (2, 1): lambda: z_forward(0, 1),
-        (2, 4): lambda: z_gather2(1, 1),
-        (2, 5): lambda: z_gather2(3, 1),
-        (2, 6): lambda: z_gather2(2, 1),
-        (2, 7): lambda: z_last(3, 0),
-        (3, 0): lambda: z_last(1, 0),
-        (3, 1): lambda: z_last(2, 0),
-        (3, 2): lambda: z_last(0, 1),
-        (3, 7): lambda: z_forward(3, 1),
+        (0, 0): lambda: z_sum2(0),
+        (0, 5): lambda: z_sum1(1),
+        (1, 1): lambda: z_forward(0, 0),
+        (1, 4): lambda: z_gather2(1, 0),
+        (1, 5): lambda: z_gather2(3, 0),
+        (1, 6): lambda: z_gather2(2, 0),
+        (2, 0): lambda: z_sum2(1),
+        (2, 1): lambda: z_last(0, 0),
+        (2, 7): lambda: z_forward(3, 0),
+        (3, 0): lambda: z_forward(1, 0),
+        (3, 1): lambda: z_forward(2, 0),
+        (3, 2): lambda: z_forward(0, 1),
+        (3, 3): lambda: z_gather2(1, 1),
+        (3, 4): lambda: z_gather2(3, 1),
+        (3, 5): lambda: z_gather2(2, 1),
+        (3, 7): lambda: z_last(3, 0),
     }
 
     def hook(k, part):
@@ -654,11 +636,17 @@
         send(nr1.at[0], nr1.at[e + 1], peer(dx, dz), nr1.at[e + 1])
         for e, (dx, dz) in enumerate(plane)
     ]
+    z_last(1, 0)
+    z_last(2, 0)
+    z_last(0, 1)
+    z_forward(3, 1)
     z_forward(1, 1)
     own_left = jnp.concatenate([left2[0, my_rows, :], left2[1, my_rows, :]], axis=1)
     ortho = (dotb(own_left, w_hi, ((1,), (1,))) + dotb(own_left, w_lo, ((1,), (1,)))).astype(BF)
     z_forward(2, 1)
-    feed[...] = (dotb(ortho, w_hi, ((1,), (0,))) + dotb(ortho, w_lo, ((1,), (0,)))).astype(BF)
+    lhs_ref[:LOCAL, :] = (
+        dotb(ortho, w_hi, ((1,), (0,))) + dotb(ortho, w_lo, ((1,), (0,)))
+    ).astype(BF)
     for wait in norm_in:
         wait()
     nr2[0] = tree([nr1[e] for e in range(16)])
@@ -668,15 +656,6 @@
     ]
     for d in (3, 1, 2):
         z_last(d, 1)
-    for _, wait in zs.values():
-        wait()
-
-    for wait in swap_sent:
-        wait()
-    for n in range(COLS // 512):
-        at = pl.ds(512 * n, 512)
-        prod = dotb(feed[...], zt_ref[at, :], ((1,), (1,)))
-        buf_ref[:, at] = (buf_ref[:, at].astype(F32) - 0.2 * prod).astype(BF)
     for wait in norm_in:
         wait()
     total = tree([nr2[f] for f in range(8)])
@@ -686,10 +665,12 @@
     lane16 = lax.broadcasted_iota(jnp.int32, (16, RANK), 1)
     pick = jnp.where(lane16 == sub16 + r * 16, scale, 0.0)
     o_hi, o_lo = split(jnp.concatenate([ortho.astype(F32) * scale, pick], axis=0))
-    lhs_ref[...] = (
+    lhs_ref[LOCAL:, :] = (
         dotb(o_hi, w_hi, ((1,), (0,)))
         + (dotb(o_hi, w_lo, ((1,), (0,))) + dotb(o_lo, w_hi, ((1,), (0,))))
     ).astype(BF)
+    for _, wait in zs.values():
+        wait()
     for wait in sent:
         wait()
 
@@ -709,9 +690,9 @@
         ((2, LOCAL, 256), BF),
         ((2, 3, 96, 256), BF),
         ((2, 2 * LOCAL, 256), BF),
-        ((10, B, B), F32),
-        ((15, 5, 8, B), F32),
-        ((10, B, B), F32),
+        ((12, B, B), BF),
+        ((15, 3, 16, B), BF),
+        ((12, B, B), BF),
         ((RANK, RANK), F32),
         ((B, B), F32),
         ((2, 4, 2, SEG // 2, 256), BF),
@@ -724,14 +705,13 @@
         ((8, 8, B), F32),
         ((2, 256, RANK), BF),
         ((2 * LOCAL, RANK), BF),
-        ((LOCAL, RANK), BF),
     ]
     return pl.pallas_call(
         gather_kernel,
         out_shape=(
             pltpu.VMEM((LOCAL, COLS), BF),
             pltpu.VMEM((COLS, RANK), BF),
-            pltpu.VMEM((LOCAL + 16, RANK), BF),
+            pltpu.VMEM((2 * LOCAL + 16, RANK), BF),
         ),
         in_specs=[anyspace] * 3,
         out_specs=(vmem,) * 3,
@@ -748,27 +728,29 @@
     )(momentum, gradient, basis)
 
 
-def apply_kernel(mom_ref, zt_ref, lhs_ref, mom_hbm, bas_hbm, upd_hbm, bas, upd, sem):
-    first = pltpu.make_async_copy(mom_ref, mom_hbm, sem.at[0])
-    first.start()
+def apply_kernel(buf_ref, zt_ref, lhs_ref, mom_hbm, bas_hbm, upd_hbm, mom, bas, upd, sem):
     factor = math.sqrt(ROWS * WIDTH / RANK)
     copies = []
+
+    def write(n, src, dst):
+        copies.append(pltpu.make_async_copy(src, dst, sem.at[n]))
+        copies[-1].start()
+
     for n in range(COLS // 512):
         at = pl.ds(512 * n, 512)
         prod = dotb(lhs_ref[...], zt_ref[at, :], ((1,), (1,)))
-        upd[:, at] = (factor * prod[:LOCAL]).astype(BF)
-        bas[:, at] = prod[LOCAL:].astype(BF)
-        copies.append(pltpu.make_async_copy(upd.at[:, at], upd_hbm.at[:, at], sem.at[n + 2]))
-        copies[-1].start()
-    copies.append(pltpu.make_async_copy(bas, bas_hbm, sem.at[1]))
-    copies[-1].start()
-    first.wait()
+        mom[:, at] = (buf_ref[:, at].astype(F32) - 0.2 * prod[:LOCAL]).astype(BF)
+        write(2 * n, mom.at[:, at], mom_hbm.at[:, at])
+        upd[:, at] = (factor * prod[LOCAL : 2 * LOCAL]).astype(BF)
+        write(2 * n + 1, upd.at[:, at], upd_hbm.at[:, at])
+        bas[:, at] = prod[2 * LOCAL :].astype(BF)
+    write(2 * (COLS // 512), bas, bas_hbm)
     for copy in copies:
         copy.wait()
 
 
-def apply_call(mom, zt, lhs):
-    held = [pltpu.with_memory_space_constraint(v, pltpu.VMEM) for v in (mom, zt, lhs)]
+def apply_call(buf, zt, lhs):
+    held = [pltpu.with_memory_space_constraint(v, pltpu.VMEM) for v in (buf, zt, lhs)]
     return pl.pallas_call(
         apply_kernel,
         out_shape=(
@@ -779,11 +761,12 @@
         in_specs=[pl.BlockSpec(memory_space=pltpu.VMEM)] * 3,
         out_specs=[pl.BlockSpec(memory_space=pl.ANY)] * 3,
         scratch_shapes=[
+            pltpu.VMEM((LOCAL, COLS), BF),
             pltpu.VMEM((16, COLS), BF),
             pltpu.VMEM((LOCAL, COLS), BF),
-            pltpu.SemaphoreType.DMA((2 + COLS // 512,)),
+            pltpu.SemaphoreType.DMA((1 + 2 * (COLS // 512),)),
         ],
-        compiler_params=pltpu.CompilerParams(vmem_limit_bytes=24 << 20),
+        compiler_params=pltpu.CompilerParams(vmem_limit_bytes=30 << 20),
         name="apply",
     )(*held)
 

time: 112 us -> 108 us (0.964)
  Pallas kernels: 111 us -> 107 us
    pallas_call x1, Pallas kernels: 107 us -> 100 us  [gather_call(): pl.pallas_call(gather_kernel, out_shape=(pltpu.VMEM((LOCAL, COLS), BF), p...]
    pallas_call x1, Pallas kernels: 4.03 us -> 6.66 us  [apply_call(): pl.pallas_call(apply_kernel, out_shape=(jax.ShapeDtypeStruct((LOCAL, COLS...]
where the time goes in v4:
time: 108 us
  Pallas kernels  107 us (99%)
    pallas_call x1, Pallas kernels, gather_call(): pl.pallas_call(gather_kernel, out_shape=(pltpu.VMEM((LOCAL, COLS), BF), p...  100 us
    pallas_call x1, Pallas kernels, apply_call(): pl.pallas_call(apply_kernel, out_shape=(jax.ShapeDtypeStruct((LOCAL, COLS...  6.66 us

profile of v4, /device:TPU:1, one launch (start us, length us, event | category | flops | bytes accessed | tf_op | source)
XLA Modules:
  0.0 107.9 jit_solution(16207063961101667911)
XLA Ops:
  0.6 100.4 %project.1 = (bf16[384,6656]{1,0:T(8,128)(2,1)S(1)}, bf16[6656,512]{1,0:T(8,128)(2,1)S(1)}, bf16[784,512]{1,0:T(8,128)(2,1)S(1)}) custom-call(bf16[384,6656]{1,0:T(8,128)(2,1)} %m_hbm.1, bf16[384,6656]{1,0:T(8,128)(2,1)} %g_hbm.1, bf16[16,6656]{1,0:T(8,128)(2,1)} %basis_hbm.1), custom_call_target="tpu_custom_call" | custom-call | tf_op jit(solution)/shard_map/project/pallas_call | solution.py:709
  101.1 6.7 %apply.1 = (bf16[384,6656]{1,0:T(8,128)(2,1)}, bf16[16,6656]{1,0:T(8,128)(2,1)}, bf16[384,6656]{1,0:T(8,128)(2,1)}) custom-call(bf16[384,6656]{1,0:T(8,128)(2,1)S(1)} %get-tuple-element.6.buf_ref, bf16[6656,512]{1,0:T(8,128)(2,1)S(1)} %get-tuple-element.7.zt_ref, bf16[784,512]{1,0:T(8,128)(2,1)S(1)} %get-tuple-element.8.lhs_ref), custom_call_target="tpu_custom_call" | custom-call | tf_op jit(solution)/shard_map/apply/pallas_call | solution.py:754

commit v5 on v4

--- a/solution.py
+++ b/solution.py
@@ -186,6 +186,11 @@
         start()
         return wait
 
+    def drain(n):
+        for wait in sent[:n]:
+            wait()
+        del sent[:n]
+
     def columns(core, part):
         return pl.ds(pl.multiple_of(core * HALF + part * PART, 128), PART)
 
@@ -316,8 +321,6 @@
         ref = half_piece(a, at2(1), n, 1)
         last[n].append(send(ref, ref, a2m, half_piece(a, at2(2), n, 1)))
 
-    ranks = [pl.ds(0, 256), pl.ds(256, 256)]
-
     def sub_rows(a, b):
         return rows_at(c * HALF + a * SEG + b * SUB, SUB)
 
@@ -325,9 +328,9 @@
         return rows_at(c * HALF + a * SEG + b * SUB + 112 * h, 112 - 16 * h)
 
     def to_sib(a, d, s):
-        ref = zt_ref.at[sub_rows(at1(a), at2(d)), ranks[s]]
+        ref = zt_ref.at[s, sub_rows(at1(a), at2(d))]
         start = (1 - c) * HALF + at2(a) * SEG + at1(d) * SUB
-        return plan(ref, ref, sib, zt_ref.at[rows_at(start, SUB), ranks[s]])
+        return plan(ref, ref, sib, zt_ref.at[s, rows_at(start, SUB)])
 
     def part(b, s):
         return zp.at[s, 0, lax.div(b, 2), rows_at(lax.rem(b, 2) * SUB, SUB)]
@@ -336,10 +339,10 @@
     for s in range(2):
 
         def sub(a, b, s=s):
-            return zt_ref.at[sub_rows(a, b), ranks[s]]
+            return zt_ref.at[s, sub_rows(a, b)]
 
         def half(a, b, h, s=s):
-            return zt_ref.at[sub_half(a, b, h), ranks[s]]
+            return zt_ref.at[s, sub_half(a, b, h)]
 
         own = sub(p1, p2)
         for d in (2, 1, 3):
@@ -387,7 +390,7 @@
         total = zp[s, 0, lax.div(p2, 2), rows_at(lax.rem(p2, 2) * SUB, SUB), :].astype(F32)
         for d in range(3):
             total = total + zr2[s, d].astype(F32)
-        zt_ref[sub_rows(p1, p2), ranks[s]] = total.astype(BF)
+        zt_ref[s, sub_rows(p1, p2), :] = total.astype(BF)
         for d in (2, 1, 3):
             z3[s, d][0]()
         z_out(0, s)
@@ -528,10 +531,11 @@
     left_pair(1)
     left_sum(1)
     left_spread(0)
+    gather_sends = len(sent)
     left_spread(1)
+    drain(gather_sends)
     left_done(0)
     z_first(0)
-    z_middle(0)
     left_done(1)
 
     blocks = [(i, j) for i in range(4) for j in range(i, 4)]
@@ -555,10 +559,10 @@
     for e, (dx, dz) in enumerate(plane):
         to = tile(mod4(x + dx) * 4 + mod4(z + dz))
         gram_in.append(send(gs.at[to], gr.at[e], peer(dx, dz), gr.at[e]))
+    z_middle(0)
     z_prepare(0)
     z_add(0)
     z_first(1)
-    z_middle(1)
     for wait in gram_in:
         wait()
     mine = tile(x * 4 + z)
@@ -567,6 +571,7 @@
     for dx, dz in plane:
         ref = gram.at[mine]
         gathered.append(send(ref, ref, peer(dx, dz), gram.at[tile(source_chip(dx, dz))]))
+    z_middle(1)
     z_prepare(1)
     z_own(0)
     z_own(1)
@@ -616,19 +621,17 @@
             if which == part:
                 pl.when(k == at)(step)
 
+    sum_sends = len(sent)
     chol_inv(tmat, wmat, hook)
     ri = lax.broadcasted_iota(jnp.int32, (RANK, RANK), 0)
     ci = lax.broadcasted_iota(jnp.int32, (RANK, RANK), 1)
     tmat[...] = jnp.where(ci <= ri, tmat[...], 0.0) * jnp.concatenate(across, axis=1)
-    w_hi, w_lo = [
-        jnp.concatenate(
-            [dotb(w, onehot[n], ((1,), (1,))).astype(BF) for n in range(2)], axis=1
-        )
-        for w in split(tmat[...])
-    ]
-
-    shard = zt_ref[sub_rows(p1, p2), :]
-    right = dotb(shard, w_hi, ((1,), (1,))) + dotb(shard, w_lo, ((1,), (1,)))
+    true_hi, true_lo = split(tmat[...])
+    shard = (
+        dotb(zt_ref[0, sub_rows(p1, p2), :], onehot[0], ((1,), (0,)))
+        + dotb(zt_ref[1, sub_rows(p1, p2), :], onehot[1], ((1,), (0,)))
+    ).astype(BF)
+    right = dotb(shard, true_hi, ((1,), (1,))) + dotb(shard, true_lo, ((1,), (1,)))
     squares = jnp.sum(right * right, axis=0, keepdims=True)
     rows = [squares[:, B * i : B * i + B] for i in range(4)] + [jnp.zeros((4, B), F32)]
     nr1[0] = jnp.concatenate(rows, axis=0)
@@ -636,6 +639,13 @@
         send(nr1.at[0], nr1.at[e + 1], peer(dx, dz), nr1.at[e + 1])
         for e, (dx, dz) in enumerate(plane)
     ]
+    w_hi, w_lo = [
+        jnp.concatenate(
+            [dotb(w, onehot[n], ((1,), (1,))).astype(BF) for n in range(2)], axis=1
+        )
+        for w in (true_hi, true_lo)
+    ]
+
     z_last(1, 0)
     z_last(2, 0)
     z_last(0, 1)
@@ -647,6 +657,7 @@
     lhs_ref[:LOCAL, :] = (
         dotb(ortho, w_hi, ((1,), (0,))) + dotb(ortho, w_lo, ((1,), (0,)))
     ).astype(BF)
+    drain(sum_sends)
     for wait in norm_in:
         wait()
     nr2[0] = tree([nr1[e] for e in range(16)])
@@ -710,7 +721,7 @@
         gather_kernel,
         out_shape=(
             pltpu.VMEM((LOCAL, COLS), BF),
-            pltpu.VMEM((COLS, RANK), BF),
+            pltpu.VMEM((2, COLS, 256), BF),
             pltpu.VMEM((2 * LOCAL + 16, RANK), BF),
         ),
         in_specs=[anyspace] * 3,
@@ -738,7 +749,8 @@
 
     for n in range(COLS // 512):
         at = pl.ds(512 * n, 512)
-        prod = dotb(lhs_ref[...], zt_ref[at, :], ((1,), (1,)))
+        prod = dotb(lhs_ref[:, :256], zt_ref[0, at, :], ((1,), (1,)))
+        prod = prod + dotb(lhs_ref[:, 256:], zt_ref[1, at, :], ((1,), (1,)))
         mom[:, at] = (buf_ref[:, at].astype(F32) - 0.2 * prod[:LOCAL]).astype(BF)
         write(2 * n, mom.at[:, at], mom_hbm.at[:, at])
         upd[:, at] = (factor * prod[LOCAL : 2 * LOCAL]).astype(BF)

time: 108 us -> 108 us (level)
  no operation moved by 1% of the time
where the time goes in v5:
time: 108 us
  Pallas kernels  107 us (99%)
    pallas_call x1, Pallas kernels, gather_call(): pl.pallas_call(gather_kernel, out_shape=(pltpu.VMEM((LOCAL, COLS), BF), p...  100 us
    pallas_call x1, Pallas kernels, apply_call(): pl.pallas_call(apply_kernel, out_shape=(jax.ShapeDtypeStruct((LOCAL, COLS...  6.66 us

profile of v5, /device:TPU:1, one launch (start us, length us, event | category | flops | bytes accessed | tf_op | source)
XLA Modules:
  0.0 107.8 jit_solution(15133551258130363531)
XLA Ops:
  0.6 100.4 %project.1 = (bf16[384,6656]{1,0:T(8,128)(2,1)S(1)}, bf16[2,6656,256]{2,1,0:T(8,128)(2,1)S(1)}, bf16[784,512]{1,0:T(8,128)(2,1)S(1)}) custom-call(bf16[384,6656]{1,0:T(8,128)(2,1)} %m_hbm.1, bf16[384,6656]{1,0:T(8,128)(2,1)} %g_hbm.1, bf16[16,6656]{1,0:T(8,128)(2,1)} %basis_hbm.1), custom_call_target="tpu_custom_call" | custom-call | tf_op jit(solution)/shard_map/project/pallas_call | solution.py:720
  101.0 6.7 %apply.1 = (bf16[384,6656]{1,0:T(8,128)(2,1)}, bf16[16,6656]{1,0:T(8,128)(2,1)}, bf16[384,6656]{1,0:T(8,128)(2,1)}) custom-call(bf16[384,6656]{1,0:T(8,128)(2,1)S(1)} %get-tuple-element.6.buf_ref, bf16[2,6656,256]{2,1,0:T(8,128)(2,1)S(1)} %get-tuple-element.7.zt_ref, bf16[784,512]{1,0:T(8,128)(2,1)S(1)} %get-tuple-element.8.lhs_ref), custom_call_target="tpu_custom_call" | custom-call | tf_op jit(solution)/shard_map/apply/pallas_call | solution.py:766
